TPU v7x, 32 devices: a whole 2x2x4 slice. The times are simulated.
32 devices in a mesh: seq: 16 (over z, y, x), exp: 2 (over core).
Axes of the slice: x: 2, y: 2, z: 4, core: 2. Of those that a mesh axis runs over, the one named last changes fastest.
Arguments:
- query_input: bfloat16 [2048, 2048], P('seq', 'exp'), may hold values from -4.5 to 4.5
- key_input: bfloat16 [2048, 2048], P('seq', 'exp'), may hold values from -4.5 to 4.5
- value_input: bfloat16 [2048, 2048], P('seq', 'exp'), may hold values from -6 to 6
- segment_ids: int32 [2048], P('seq'), may hold values from 0 to 15, never falling along the last dimension, each value on 1 to 256 neighbouring positions
- residual_in: bfloat16 [2048, 4096], P('seq', 'exp'), may hold values from -13.5 to 13.5
- out_weight: bfloat16 [2048, 4096], P('exp'), may hold values from -0.1875 to 0.1875
- norm_gain: float32 [4096], P('exp'), may hold values from 0.1 to 1.9
- router: bfloat16 [4096, 32], P(None, 'seq'), may hold values from -0.1875 to 0.1875
- modality: int32 [2048], P('seq'), may hold values from 0 to 1
- expert_in: int32 [2048], P('seq'), may hold values from 0 to 15, as said below
- gate_weight: bfloat16 [32, 4096, 2816], P('seq', None, 'exp'), may hold values from -0.09375 to 0.09375
- up_weight: bfloat16 [32, 4096, 2816], P('seq', None, 'exp'), may hold values from -0.09375 to 0.09375
- down_weight: bfloat16 [32, 2816, 4096], P('seq', 'exp'), may hold values from -0.15625 to 0.15625
Outputs:
- layer_out: bfloat16 [2048, 4096], P('seq', 'exp')
Inputs may be any that keep to these rules, and one draw needn't show every extreme that they name: `segment_ids`: document numbers never fall along the sequence, and a document holds at most an eighth of the 2048 tokens. `expert_in`: within each aligned block of 128 tokens no expert (modality and number together) is chosen by more than 7 tokens, and in every block some expert is chosen by exactly 7.
All inputs are finite; a program needn't handle non-finite values.
Results may differ from a plain program's by a relative error of at most 0.0095.
Values may be sent and summed in bfloat16 or wider, within the bound.
No kernel may reach another device: no remote copies, remote signals or barrier semaphores. Data moves between devices by JAX's collectives and lax.ppermute only.
A program may use at most 128 MiB of HBM per device.

v0:
```python
import jax
import jax.numpy as jnp
from jax import lax
from jax.sharding import PartitionSpec as P

D = 4096
HEAD_DIM = 128
EXPERTS = 32
MODAL_EXPERTS = 16
CAPACITY = 7


NEGATIVE = -1e30
EPSILON = 1e-05


def passed_along(value, axis, steps):
    count = lax.axis_size(axis)
    leading, last = (max(0, -steps), min(count, count - steps))
    return lax.ppermute(value, axis, [(source, source + steps) for source in range(leading, last)])


def absorb(carry_state, query_heads, key_block, value_block, allowed):
    running_max, denominators, numerators = carry_state
    scores = jnp.einsum(
        "qhd,khd->hqk", query_heads, key_block, preferred_element_type=jnp.float32
    ) * HEAD_DIM ** (-0.5)
    masked = jnp.where(allowed[None], scores, NEGATIVE)
    new_max = jnp.maximum(running_max, jnp.max(masked, axis=2))
    rescale = jnp.exp(running_max - new_max)
    weights = jnp.exp(masked - new_max[:, :, None])
    denominators = denominators * rescale + jnp.sum(weights, axis=2)
    numerators = numerators * rescale[:, :, None] + jnp.einsum(
        "hqk,khd->hqd",
        weights.astype(jnp.bfloat16),
        value_block,
        preferred_element_type=jnp.float32,
    )
    return (new_max, denominators, numerators)


def local(
    query_input,
    key_input,
    value_input,
    segment_ids,
    residual_in,
    out_weight,
    norm_gain,
    router,
    modality,
    expert_in,
    gate_weight,
    up_weight,
    down_weight,
):
    token_count = query_input.shape[0]
    head_count = query_input.shape[1] // HEAD_DIM
    query_heads = query_input.reshape(token_count, head_count, HEAD_DIM)
    key_heads = key_input.reshape(token_count, head_count, HEAD_DIM)
    value_heads = value_input.reshape(token_count, head_count, HEAD_DIM)
    positions = jnp.arange(token_count, dtype=jnp.int32)
    local_mask = (segment_ids[:, None] == segment_ids[None, :]) & (
        positions[None, :] <= positions[:, None]
    )
    empty_state = (
        jnp.full((head_count, token_count), NEGATIVE, jnp.float32),
        jnp.zeros((head_count, token_count), jnp.float32),
        jnp.zeros((head_count, token_count, HEAD_DIM), jnp.float32),
    )
    carry_state = absorb(empty_state, query_heads, key_heads, value_heads, local_mask)
    cycle_index = lax.axis_index("seq")

    def visit(step_number, loop_carry):
        visit_state, key_block, value_block, travel_segments = loop_carry
        key_block, value_block, travel_segments = passed_along(
            (key_block, value_block, travel_segments), "seq", 1
        )
        has_block = cycle_index - step_number - 1 >= 0
        allowed = has_block & (segment_ids[:, None] == travel_segments.astype(jnp.int32)[None, :])
        visit_state = absorb(visit_state, query_heads, key_block, value_block, allowed)
        return (visit_state, key_block, value_block, travel_segments)

    start_carry = (carry_state, key_heads, value_heads, segment_ids.astype(jnp.bfloat16))
    final_carry = lax.fori_loop(0, lax.axis_size("seq") // 8, visit, start_carry)
    running_max, denominators, numerators = final_carry[0]
    attended = (numerators / denominators[:, :, None]).astype(jnp.bfloat16)
    attended = jnp.transpose(attended, (1, 0, 2)).reshape(token_count, head_count * HEAD_DIM)
    projected = jnp.dot(attended, out_weight, preferred_element_type=jnp.float32)
    attention = lax.psum_scatter(
        projected.astype(jnp.bfloat16), "exp", scatter_dimension=1, tiled=True
    ).astype(jnp.float32)
    residual = residual_in.astype(jnp.float32) + attention
    squares = jnp.sum(residual * residual, axis=1)
    square_total = lax.psum(squares, "exp")
    normed = (residual * lax.rsqrt(square_total / D + EPSILON)[:, None] * norm_gain).astype(
        jnp.bfloat16
    )
    picked = modality * MODAL_EXPERTS + expert_in
    one_hot = (picked[:, None] == jnp.arange(EXPERTS, dtype=jnp.int32)[None, :]).astype(jnp.int32)
    rank_in_block = jnp.sum(one_hot * (jnp.cumsum(one_hot, axis=0) - 1), axis=1)
    slot_index = picked * CAPACITY + rank_in_block
    outgoing = (
        jnp.zeros((EXPERTS * CAPACITY, normed.shape[1]), jnp.bfloat16).at[slot_index].set(normed)
    )
    sliced = lax.all_to_all(
        outgoing.reshape(EXPERTS, CAPACITY, normed.shape[1]),
        "seq",
        split_axis=0,
        concat_axis=1,
        tiled=True,
    )
    arrived = lax.all_gather(sliced, "exp", axis=2, tiled=True)
    gate_sum = jnp.einsum("erd,edf->erf", arrived, gate_weight, preferred_element_type=jnp.float32)
    up_sum = jnp.einsum("erd,edf->erf", arrived, up_weight, preferred_element_type=jnp.float32)
    logits = jnp.einsum("erd,de->er", arrived, router, preferred_element_type=jnp.float32)
    hidden = (jax.nn.silu(gate_sum) * up_sum * jax.nn.sigmoid(logits)[:, :, None]).astype(
        jnp.bfloat16
    )
    partial_value = jnp.einsum(
        "erf,efd->erd", hidden, down_weight, preferred_element_type=jnp.float32
    )
    summed = lax.psum_scatter(
        partial_value.astype(jnp.bfloat16), "exp", scatter_dimension=2, tiled=True
    )
    returned = lax.all_to_all(summed, "seq", split_axis=1, concat_axis=0, tiled=True)
    routed = returned.reshape(EXPERTS * CAPACITY, returned.shape[2])[slot_index]
    return (residual + routed.astype(jnp.float32)).astype(jnp.bfloat16)


def solution(mesh):
    in_specs = (
        P("seq", "exp"),
        P("seq", "exp"),
        P("seq", "exp"),
        P("seq"),
        P("seq", "exp"),
        P("exp", None),
        P("exp"),
        P(None, "seq"),
        P("seq"),
        P("seq"),
        P("seq", None, "exp"),
        P("seq", None, "exp"),
        P("seq", "exp", None),
    )
    out_specs = P("seq", "exp")
    return jax.shard_map(local, mesh=mesh, in_specs=in_specs, out_specs=out_specs, check_vma=False)
```

profile of v0, /device:TPU:0, one launch (start us, length us, event | category | flops | bytes accessed | tf_op | source)
XLA Modules:
  0.0 196.0 jit_solution(5187522884517526720)
XLA Ops:
  6.5 0.8 fusion.26
  7.4 0.7 convert_element_type.58
  8.0 1.2 copy.35
  9.2 1.1 copy.36
  11.9 32.7 %while.25 = (s32[]{:T(128)}, f32[8,128]{1,0:T(8,128)S(1)}, f32[8,128]{1,0:T(8,128)S(1)}, f32[8,128,128]{2,1,0:T(8,128)S(1)}, bf16[128,8,128]{2,0,1:T(8,128)(2,1)...) while((s32[]{:T(128)}, f32[8,128]{1,0:T(8,128)S(1)}, ...), condition=%wide.region_5.6_spmd, body=%wide.region_2.5_spmd.sunk | while | flops 68585600 | bytes 6688279 | solution.py:85
  11.9 4.9 %collective-permute-start.1 = (bf16[128,8,128]{2,0,1:T(8,128)(2,1)S(1)}, bf16[128,8,128]{2,0,1:T(8,128)(2,1)S(1)}, u32[]{:S(2)}, u32[]{:S(2)}) collective-permute-start(bf16[128,8,128]{2,0,1:T(8,128)(2,1)S(1)} %get-tuple-element.384), channel_id=1, source_target_pairs={{0,2},{2,4},{4,6},{6,8},{8,10},{10,12},{12,14},{14,16},{16,18},{18... | collective-permute-start | bytes 786440 | tf_op jit(solution)/shard_map/while/body/eval_jaxpr/ppermute | solution.py:20
  16.8 3.4 %collective-permute-start = (bf16[128]{0:T(256)(128)(2,1)S(1)}, bf16[128]{0:T(256)(128)(2,1)S(1)}, u32[]{:S(2)}, u32[]{:S(2)}) collective-permute-start(bf16[128]{0:T(256)(128)(2,1)S(1)} %get-tuple-element.386), channel_id=1, source_target_pairs={{0,2},{2,4},{4,6},{6,8},{8,10},{10,12},{12,14},{14,16},{16,18},{18... | collective-permute-start | bytes 776 | tf_op jit(solution)/shard_map/while/body/eval_jaxpr/ppermute | solution.py:20
  20.1 3.4 %collective-permute-start.2 = (bf16[128,8,128]{2,0,1:T(8,128)(2,1)S(1)}, bf16[128,8,128]{2,0,1:T(8,128)(2,1)S(1)}, u32[]{:S(2)}, u32[]{:S(2)}) collective-permute-start(bf16[128,8,128]{2,0,1:T(8,128)(2,1)S(1)} %get-tuple-element.385), channel_id=1, source_target_pairs={{0,2},{2,4},{4,6},{6,8},{8,10},{10,12},{12,14},{14,16},{16,18},{18... | collective-permute-start | bytes 786440 | tf_op jit(solution)/shard_map/while/body/eval_jaxpr/ppermute | solution.py:20
  24.2 4.3 %collective-permute-done.2 = bf16[128,8,128]{2,0,1:T(8,128)(2,1)S(1)} collective-permute-done((bf16[128,8,128]{2,0,1:T(8,128)(2,1)S(1)}, bf16[128,8,128]{2,0,1:T(8,128)(2,1)S(1)}, u32[]{:S(2)}, u32[]{:S(2)}) %collective-permute-start.2) | collective-permute-done | bytes 262176 | tf_op jit(solution)/shard_map/while/body/eval_jaxpr/ppermute | solution.py:20
  28.6 0.4 convolution_add_fusion.3
  29.0 4.4 %collective-permute-start.1 = (bf16[128,8,128]{2,0,1:T(8,128)(2,1)S(1)}, bf16[128,8,128]{2,0,1:T(8,128)(2,1)S(1)}, u32[]{:S(2)}, u32[]{:S(2)}) collective-permute-start(bf16[128,8,128]{2,0,1:T(8,128)(2,1)S(1)} %get-tuple-element.384), channel_id=1, source_target_pairs={{0,2},{2,4},{4,6},{6,8},{8,10},{10,12},{12,14},{14,16},{16,18},{18... | collective-permute-start | bytes 786440 | tf_op jit(solution)/shard_map/while/body/eval_jaxpr/ppermute | solution.py:20
  33.4 4.3 %collective-permute-start = (bf16[128]{0:T(256)(128)(2,1)S(1)}, bf16[128]{0:T(256)(128)(2,1)S(1)}, u32[]{:S(2)}, u32[]{:S(2)}) collective-permute-start(bf16[128]{0:T(256)(128)(2,1)S(1)} %get-tuple-element.386), channel_id=1, source_target_pairs={{0,2},{2,4},{4,6},{6,8},{8,10},{10,12},{12,14},{14,16},{16,18},{18... | collective-permute-start | bytes 776 | tf_op jit(solution)/shard_map/while/body/eval_jaxpr/ppermute | solution.py:20
  37.7 2.5 %collective-permute-start.2 = (bf16[128,8,128]{2,0,1:T(8,128)(2,1)S(1)}, bf16[128,8,128]{2,0,1:T(8,128)(2,1)S(1)}, u32[]{:S(2)}, u32[]{:S(2)}) collective-permute-start(bf16[128,8,128]{2,0,1:T(8,128)(2,1)S(1)} %get-tuple-element.385), channel_id=1, source_target_pairs={{0,2},{2,4},{4,6},{6,8},{8,10},{10,12},{12,14},{14,16},{16,18},{18... | collective-permute-start | bytes 786440 | tf_op jit(solution)/shard_map/while/body/eval_jaxpr/ppermute | solution.py:20
  40.9 3.2 %collective-permute-done.2 = bf16[128,8,128]{2,0,1:T(8,128)(2,1)S(1)} collective-permute-done((bf16[128,8,128]{2,0,1:T(8,128)(2,1)S(1)}, bf16[128,8,128]{2,0,1:T(8,128)(2,1)S(1)}, u32[]{:S(2)}, u32[]{:S(2)}) %collective-permute-start.2) | collective-permute-done | bytes 262176 | tf_op jit(solution)/shard_map/while/body/eval_jaxpr/ppermute | solution.py:20
  44.9 5.7 %convolution_convert_fusion.1 = bf16[128,4096]{1,0:T(8,128)(2,1)} fusion(bf16[128,1024]{0,1:T(8,128)(2,1)S(1)} %bitcast.47, bf16[1024,4096]{1,0:T(8,128)(2,1)} %param.20), kind=kOutput, calls=%fused_computation.16 | convolution fusion | flops 1074266112 | bytes 9699328 | tf_op jit(solution)/shard_map/dot_general | solution.py:89
  51.2 11.2 %reduce-scatter.3.cloned.1.call-done = bf16[128,2048]{1,0:T(8,128)(2,1)} async-done(((bf16[128,4096]{1,0:T(8,128)(2,1)}), bf16[128,2048]{1,0:T(8,128)(2,1)}) %reduce-scatter.3.cloned.1.call-update) | async-done | bytes 524304 | tf_op jit(solution)/shard_map/reduce_scatter | solution.py:90
  62.3 1.3 multiply_reduce_fusion
  63.6 2.5 %psum.7 = f32[128]{0:T(128)S(1)} all-reduce(f32[128]{0:T(128)S(1)} %multiply_reduce_fusion), channel_id=1, replica_groups=mesh['seq'=16,'exp'=2] {'exp'}, use_global_device_ids=true, to_apply=%region_10.11 | all-reduce | flops 128 | bytes 1024 | tf_op jit(solution)/shard_map/psum | solution.py:95
  66.1 2.3 %scatter_custom_fusion = bf16[224,2048]{1,0:T(8,128)(2,1)S(1)} fusion(s32[128]{0:T(128)S(1)} %compare_select_fusion, bf16[128,2048]{1,0:T(8,128)(2,1)} %reduce-scatter.3.cloned.1.call-done, bf16[128,2048]{1,0:T(8,128)(2,1)S(1)} %copy-done.3, f32[2048]{0:T(1024)S(1)} %copy-done.8, f32[128]{0:T(128)S(1)} %add_rsqrt_fusion, bf16[]{:T(256)} %constant.98.clone.1), kind=kCustom, calls=%fused_computation.34 | custom fusion | flops 1572864 | bytes 1974786 | tf_op jit(solution)/shard_map/scatter | solution.py:104
  68.7 33.3 %all_to_all.33 = bf16[32,7,2048]{2,1,0:T(8,128)(2,1)S(1)} all-to-all(bf16[32,7,2048]{2,1,0:T(8,128)(2,1)S(1)} %reshape.105), channel_id=1, replica_groups=mesh['seq'=16,'exp'=2] {'seq'}, dimensions={0} | all-to-all | bytes 1835008 | tf_op jit(solution)/shard_map/all_to_all | solution.py:106
  102.0 1.0 copy.59
  103.0 1.2 copy.48
  104.5 8.6 %all-gather.2.cloned.1.call-done = bf16[2,112,4096]{2,1,0:T(8,128)(2,1)} async-done(((bf16[2,112,2048]{2,1,0:T(8,128)(2,1)}), bf16[2,112,4096]{2,1,0:T(8,128)(2,1)}) %all-gather.2.cloned.1.call-update) | async-done | bytes 1835024 | tf_op jit(solution)/shard_map/all_gather | solution.py:113
  113.0 2.2 %fusion.27 = f32[2,1,112]{2,1,0:T(1,128)S(1)} fusion(bf16[2,112,4096]{2,1,0:T(8,128)(2,1)} %all-gather.2.cloned.1.call-done, bf16[4096,2,1]{0,1,2:T(2,128)(2,1)S(1)} %bitcast.37), kind=kOutput, calls=%fused_computation.48 | convolution fusion | flops 1835008 | bytes 1852288 | tf_op jit(solution)/shard_map/erd,de->er/dot_general | solution.py:116
  115.3 9.4 %fusion.32 = f32[2,112,1408]{2,1,0:T(8,128)S(1)} fusion(bf16[2,112,4096]{2,1,0:T(8,128)(2,1)S(1)} %copy-done.2, bf16[2,4096,1408]{2,1,0:T(8,128)(2,1)} %param.25), kind=kOutput, calls=%fused_computation.60 | convolution fusion | flops 2583691264 | bytes 26165248 | tf_op jit(solution)/shard_map/erd,edf->erf/dot_general | solution.py:114
  124.7 18.9 %convolution_convert_fusion = bf16[2,112,4096]{2,1,0:T(8,128)(2,1)} fusion(bf16[2,1408,4096]{2,1,0:T(8,128)(2,1)} %param.27, bf16[2,112,4096]{2,1,0:T(8,128)(2,1)S(1)} %copy-done.2, bf16[2,4096,1408]{2,1,0:T(8,128)(2,1)} %param.26, f32[2,112,1408]{2,1,0:T(8,128)S(1)} %fusion.32, f32[2,112]{1,0:T(2,128)S(1)} %add_divide_fusion), kind=kOutput, calls=%fused_computation.15 | convolution fusion | flops 5170507776 | bytes 51069824 | tf_op jit(solution)/shard_map/erf,efd->erd/dot_general | solution.py:120
  143.7 10.7 %reduce-scatter.5.cloned.1.call-done = bf16[2,112,2048]{2,1,0:T(8,128)(2,1)} async-done(((bf16[2,112,4096]{2,1,0:T(8,128)(2,1)}), bf16[2,112,2048]{2,1,0:T(8,128)(2,1)}) %reduce-scatter.5.cloned.1.call-update) | async-done | bytes 917520 | tf_op jit(solution)/shard_map/reduce_scatter | solution.py:123
  154.4 3.0 %copy.49 = bf16[2,112,2048]{2,0,1:T(2,128)(2,1)} copy(bf16[2,112,2048]{2,1,0:T(8,128)(2,1)} %reduce-scatter.5.cloned.1.call-done) | data formatting | bytes 1835008 | tf_op jit(solution)/shard_map/reduce_scatter | solution.py:123
  157.4 6.8 %all-to-all-start.1 = ((bf16[2,112,2048]{2,0,1:T(2,128)(2,1)}), bf16[2,112,2048]{2,0,1:T(2,128)(2,1)S(1)}, u32[]{:S(2)}, u32[]{:S(2)}) async-start(bf16[2,112,2048]{2,0,1:T(2,128)(2,1)} %copy.49), calls=%async_computation.3 | async-start | bytes 1835008 | tf_op jit(solution)/shard_map/all_to_all | solution.py:126
  164.2 22.4 %all-to-all-done.1 = bf16[2,112,2048]{2,0,1:T(2,128)(2,1)S(1)} async-done(((bf16[2,112,2048]{2,0,1:T(2,128)(2,1)}), bf16[2,112,2048]{2,0,1:T(2,128)(2,1)S(1)}, u32[]{:S(2)}, u32[]{:S(2)}) %all-to-all-start.1) | async-done | bytes 917536 | tf_op jit(solution)/shard_map/all_to_all | solution.py:126
  187.3 0.9 gather_fusion
  188.4 1.0 add_convert_fusion
  (75 shorter events, 5.3 us)
Async XLA Ops:
  6.5 106.5 %copy-start = (bf16[4096,2]{0,1:T(2,128)(2,1)S(1)}, bf16[4096,2]{0,1:T(2,128)(2,1)}, u32[]{:S(2)}) copy-start(bf16[4096,2]{0,1:T(2,128)(2,1)} %param.22) | copy-start | bytes 49156
  6.5 55.8 %reduce-scatter.3.cloned.1.call-start = ((), (), s32[]{:S(2)}) async-start(), calls=%async_computation.4 | async-start | bytes 1572864 | tf_op jit(solution)/shard_map/reduce_scatter | solution.py:90
  8.0 3.1 %copy-start.6 = (bf16[128,1024]{1,0:T(8,128)(2,1)S(1)}, bf16[128,1024]{1,0:T(8,128)(2,1)}, u32[]{:S(2)}) copy-start(bf16[128,1024]{1,0:T(8,128)(2,1)} %param.17) | copy-start | bytes 786436
  10.7 1.2 copy-start.7
  11.9 11.8 %collective-permute-start.1 = (bf16[128,8,128]{2,0,1:T(8,128)(2,1)S(1)}, bf16[128,8,128]{2,0,1:T(8,128)(2,1)S(1)}, u32[]{:S(2)}, u32[]{:S(2)}) collective-permute-start(bf16[128,8,128]{2,0,1:T(8,128)(2,1)S(1)} %get-tuple-element.384), channel_id=1, source_target_pairs={{0,2},{2,4},{4,6},{6,8},{8,10},{10,12},{12,14},{14,16},{16,18},{18... | collective-permute-start | bytes 786440 | tf_op jit(solution)/shard_map/while/body/eval_jaxpr/ppermute | solution.py:20
  16.8 6.8 %collective-permute-start = (bf16[128]{0:T(256)(128)(2,1)S(1)}, bf16[128]{0:T(256)(128)(2,1)S(1)}, u32[]{:S(2)}, u32[]{:S(2)}) collective-permute-start(bf16[128]{0:T(256)(128)(2,1)S(1)} %get-tuple-element.386), channel_id=1, source_target_pairs={{0,2},{2,4},{4,6},{6,8},{8,10},{10,12},{12,14},{14,16},{16,18},{18... | collective-permute-start | bytes 776 | tf_op jit(solution)/shard_map/while/body/eval_jaxpr/ppermute | solution.py:20
  20.1 8.4 %collective-permute-start.2 = (bf16[128,8,128]{2,0,1:T(8,128)(2,1)S(1)}, bf16[128,8,128]{2,0,1:T(8,128)(2,1)S(1)}, u32[]{:S(2)}, u32[]{:S(2)}) collective-permute-start(bf16[128,8,128]{2,0,1:T(8,128)(2,1)S(1)} %get-tuple-element.385), channel_id=1, source_target_pairs={{0,2},{2,4},{4,6},{6,8},{8,10},{10,12},{12,14},{14,16},{16,18},{18... | collective-permute-start | bytes 786440 | tf_op jit(solution)/shard_map/while/body/eval_jaxpr/ppermute | solution.py:20
  29.0 11.4 %collective-permute-start.1 = (bf16[128,8,128]{2,0,1:T(8,128)(2,1)S(1)}, bf16[128,8,128]{2,0,1:T(8,128)(2,1)S(1)}, u32[]{:S(2)}, u32[]{:S(2)}) collective-permute-start(bf16[128,8,128]{2,0,1:T(8,128)(2,1)S(1)} %get-tuple-element.384), channel_id=1, source_target_pairs={{0,2},{2,4},{4,6},{6,8},{8,10},{10,12},{12,14},{14,16},{16,18},{18... | collective-permute-start | bytes 786440 | tf_op jit(solution)/shard_map/while/body/eval_jaxpr/ppermute | solution.py:20
  33.4 6.8 %collective-permute-start = (bf16[128]{0:T(256)(128)(2,1)S(1)}, bf16[128]{0:T(256)(128)(2,1)S(1)}, u32[]{:S(2)}, u32[]{:S(2)}) collective-permute-start(bf16[128]{0:T(256)(128)(2,1)S(1)} %get-tuple-element.386), channel_id=1, source_target_pairs={{0,2},{2,4},{4,6},{6,8},{8,10},{10,12},{12,14},{14,16},{16,18},{18... | collective-permute-start | bytes 776 | tf_op jit(solution)/shard_map/while/body/eval_jaxpr/ppermute | solution.py:20
  37.7 6.4 %collective-permute-start.2 = (bf16[128,8,128]{2,0,1:T(8,128)(2,1)S(1)}, bf16[128,8,128]{2,0,1:T(8,128)(2,1)S(1)}, u32[]{:S(2)}, u32[]{:S(2)}) collective-permute-start(bf16[128,8,128]{2,0,1:T(8,128)(2,1)S(1)} %get-tuple-element.385), channel_id=1, source_target_pairs={{0,2},{2,4},{4,6},{6,8},{8,10},{10,12},{12,14},{14,16},{16,18},{18... | collective-permute-start | bytes 786440 | tf_op jit(solution)/shard_map/while/body/eval_jaxpr/ppermute | solution.py:20
  44.8 5.8 %copy-start.9 = (s32[128]{0:T(128)S(1)}, s32[128]{0:T(128)}, u32[]{:S(2)}) copy-start(s32[128]{0:T(128)} %param.24) | copy-start | bytes 1540
  44.9 5.8 %copy-start.10 = (s32[128]{0:T(128)S(1)}, s32[128]{0:T(128)}, u32[]{:S(2)}) copy-start(s32[128]{0:T(128)} %param.23) | copy-start | bytes 1540
  44.9 17.5 %copy-start.3 = (bf16[128,2048]{1,0:T(8,128)(2,1)S(1)}, bf16[128,2048]{1,0:T(8,128)(2,1)}, u32[]{:S(2)}) copy-start(bf16[128,2048]{1,0:T(8,128)(2,1)} %param.19) | copy-start | bytes 1572868
  50.6 15.5 %copy-start.8 = (f32[2048]{0:T(1024)S(1)}, f32[2048]{0:T(1024)}, u32[]{:S(2)}) copy-start(f32[2048]{0:T(1024)} %param.21) | copy-start | bytes 24580
  50.6 62.4 %all-gather.2.cloned.1.call-start = ((), (), s32[]{:S(2)}) async-start(), calls=%async_computation.5 | async-start | bytes 2752512 | tf_op jit(solution)/shard_map/all_gather | solution.py:113
  104.3 50.1 %reduce-scatter.5.cloned.1.call-start = ((), (), s32[]{:S(2)}) async-start(), calls=%async_computation.6 | async-start | bytes 2752512 | tf_op jit(solution)/shard_map/reduce_scatter | solution.py:123
  113.0 2.2 %copy-start.2 = (bf16[2,112,4096]{2,1,0:T(8,128)(2,1)S(1)}, bf16[2,112,4096]{2,1,0:T(8,128)(2,1)}, u32[]{:S(2)}) copy-start(bf16[2,112,4096]{2,1,0:T(8,128)(2,1)} %all-gather.2.cloned.1.call-done) | copy-start | bytes 5505028
  157.4 29.1 %all-to-all-start.1 = ((bf16[2,112,2048]{2,0,1:T(2,128)(2,1)}), bf16[2,112,2048]{2,0,1:T(2,128)(2,1)S(1)}, u32[]{:S(2)}, u32[]{:S(2)}) async-start(bf16[2,112,2048]{2,0,1:T(2,128)(2,1)} %copy.49), calls=%async_computation.3 | async-start | bytes 1835008 | tf_op jit(solution)/shard_map/all_to_all | solution.py:126
  187.2 1.0 copy-start.4
  187.2 1.2 copy-start.5
  187.2 2.2 %copy-start.1 = (bf16[4096,2]{0,1:T(2,128)(2,1)S(1)}, bf16[4096,2]{0,1:T(2,128)(2,1)}, u32[]{:S(2)}) copy-start(bf16[4096,2]{0,1:T(2,128)(2,1)} %param.22) | copy-start | bytes 49156
Sparse Core Ops, SparseCore 0:
  50.7 11.5 reduce-scatter.2
  104.4 8.6 all-gather.1
  143.8 10.5 reduce-scatter.4
where the time goes:
time: 197 us; the launch traced here: 196 us
  waiting for transfers between devices  60.4 us (31%)
  matrix products  38.4 us (19%)
  blocking collectives  35.7 us (18%)
  starting transfers between devices  29.9 us (15%)
  between operations  13.4 us (7%)
  local copies, waits for them, and re-layouts  10.8 us (5%)
  other arithmetic  7.13 us (4%)
    all_to_all x1, blocking collectives, local(): lax.all_to_all(outgoing.reshape(EXPERTS, CAPACITY, normed.shape[1]), 'seq...  33.3 us
    ppermute x6, starting transfers between devices, passed_along(): lax.ppermute(value, axis, [(source, source + steps) for source in range(l...  22.9 us
    all_to_all x1, waiting for transfers between devices, local(): lax.all_to_all(summed, 'seq', split_axis=1, concat_axis=0, tiled=True)  22.4 us
    dot_general x1, matrix products, local(): jnp.einsum('erf,efd->erd', hidden, down_weight, preferred_element_type=jn...  18.9 us
    reduce_scatter x1, waiting for transfers between devices, local(): lax.psum_scatter(projected.astype(jnp.bfloat16), 'exp', scatter_dimension...  11.2 us
    reduce_scatter x1, waiting for transfers between devices, local(): lax.psum_scatter(partial_value.astype(jnp.bfloat16), 'exp', scatter_dimen...  10.7 us
    dot_general x1, matrix products, local(): jnp.einsum('erd,edf->erf', arrived, gate_weight, preferred_element_type=j...  9.43 us
    all_gather x1, waiting for transfers between devices, local(): arrived = lax.all_gather(sliced, 'exp', axis=2, tiled=True)  8.56 us
  transfers between devices with their start and end apart: 10, of which 6 were waited for; matrix products, arithmetic and copies ran while one was open for 1% of the time, Pallas kernels for 0%

commit v1 on v0

v1 whole, which is shorter than its diff:
```python
import functools

import jax
import jax.numpy as jnp
from jax import lax
from jax.experimental import pallas as pl
from jax.experimental.pallas import tpu as pltpu
from jax.sharding import PartitionSpec as P

HEAD_DIM = 128
MODAL_EXPERTS = 16
CAPACITY = 7
NEGATIVE = -1e30
EPSILON = 1e-05
ROWS = 16
MIB = 1 << 20

F32 = jnp.float32
BF16 = jnp.bfloat16

ANY = pl.BlockSpec(memory_space=pl.ANY)
VMEM = pl.BlockSpec(memory_space=pltpu.VMEM)


def tiles(width, size):
    return [(start, min(size, width - start)) for start in range(0, width, size)]


def dot(left, right, dims=((1,), (0,))):
    return lax.dot_general(left, right, (dims, ((), ())), preferred_element_type=F32)


def shifted(value, axis, steps):
    count = lax.axis_size(axis)
    leading, last = max(0, -steps), min(count, count - steps)
    return lax.ppermute(value, axis, [(source, source + steps) for source in range(leading, last)])


def rotated(value, axis, steps):
    count = lax.axis_size(axis)
    return lax.ppermute(value, axis, [(source, (source + steps) % count) for source in range(count)])


def cost(flops, moved):
    return pl.CostEstimate(flops=int(flops), bytes_accessed=int(moved), transcendentals=0)


def kernel_call(body, ins, out_shape, specs=None, scratch=(), flops=0, moved=0, limit=16):
    specs = specs or [VMEM] * len(ins)
    outs = jax.tree.map(lambda _: VMEM, out_shape)
    return pl.pallas_call(
        body,
        in_specs=specs,
        out_specs=outs,
        out_shape=out_shape,
        scratch_shapes=list(scratch),
        cost_estimate=cost(flops, moved),
        compiler_params=pltpu.CompilerParams(vmem_limit_bytes=limit * MIB),
    )(*ins)


def struct(shape, dtype):
    return jax.ShapeDtypeStruct(shape, dtype)


def fetch_weights(out_weight, gate_weight, up_weight, feature_count):
    group = lax.axis_size("exp")
    head_rows = out_weight.shape[0]
    experts, _, hidden = gate_weight.shape

    def body(*refs):
        out_ref, gate_ref, up_ref = refs[:3]
        sems = refs[-1]
        me = lax.axis_index("exp")
        copies = []
        for k in range(group):
            ahead = lax.rem(me + k, group)
            behind = lax.rem(me + group - k, group)
            columns = pl.ds(pl.multiple_of(ahead * feature_count, 128), feature_count)
            rows = pl.ds(pl.multiple_of(behind * feature_count, 128), feature_count)
            out_to, gate_to, up_to = refs[3:6] if k == 0 else [ref.at[k - 1] for ref in refs[6:9]]
            copies.append((out_ref.at[:, columns], out_to))
            copies.append((gate_ref.at[:, rows, :], gate_to))
            copies.append((up_ref.at[:, rows, :], up_to))
        started = [
            pltpu.make_async_copy(source, target, sems.at[index])
            for index, (source, target) in enumerate(copies)
        ]
        for copy in started:
            copy.start()
        for copy in started:
            copy.wait()

    own = (
        (head_rows, feature_count),
        (experts, feature_count, hidden),
        (experts, feature_count, hidden),
    )
    shapes = [pltpu.VMEM(shape, BF16) for shape in own]
    shapes += [pltpu.VMEM((group - 1, *shape), BF16) for shape in own]
    return kernel_call(
        body,
        (out_weight, gate_weight, up_weight),
        tuple(shapes),
        specs=[ANY] * 3,
        scratch=[pltpu.SemaphoreType.DMA((3 * group,))],
        moved=2 * (out_weight.size + gate_weight.size + up_weight.size),
        limit=1,
    )


def attend(query, blocks, query_segments, out_slices, gain_row):
    group = lax.axis_size("exp")
    tokens, columns = query.shape
    features = out_slices.shape[2]
    count = len(blocks)

    def body(*refs):
        query_ref, block_refs = refs[0], refs[1 : 1 + count]
        segments_ref, out_ref, gain_ref = refs[1 + count : 4 + count]
        attended_ref, send_refs = refs[4 + count], refs[5 + count :]
        own = segments_ref[...]
        masks = []
        for index, block in enumerate(block_refs):
            theirs = block[2 * tokens : 2 * tokens + ROWS, :tokens].astype(F32)[0:1, :]
            mask = jnp.broadcast_to(own, (tokens, tokens)) == jnp.broadcast_to(
                theirs, (tokens, tokens)
            )
            if index == 0:
                key_pos = lax.broadcasted_iota(jnp.int32, (tokens, tokens), 1)
                query_pos = lax.broadcasted_iota(jnp.int32, (tokens, tokens), 0)
                mask = mask & (key_pos <= query_pos)
            masks.append(mask)
        for head in range(columns // HEAD_DIM):
            part = slice(head * HEAD_DIM, (head + 1) * HEAD_DIM)
            heads = query_ref[:, part]
            scores = [
                jnp.where(
                    mask,
                    dot(heads, block[:tokens, part], ((1,), (1,))) * HEAD_DIM ** (-0.5),
                    NEGATIVE,
                )
                for block, mask in zip(block_refs, masks)
            ]
            peak = functools.reduce(
                jnp.maximum, [jnp.max(score, axis=1, keepdims=True) for score in scores]
            )
            weights = [jnp.exp(score - peak) for score in scores]
            total = sum(jnp.sum(weight, axis=1, keepdims=True) for weight in weights)
            summed = sum(
                dot(weight.astype(BF16), block[tokens : 2 * tokens, part])
                for weight, block in zip(weights, block_refs)
            )
            attended_ref[:, part] = (summed / total).astype(BF16)
        high = gain_ref[...].astype(BF16)
        low = (gain_ref[...] - high.astype(F32)).astype(BF16)
        row = lax.broadcasted_iota(jnp.int32, (ROWS, features), 0)
        gains = jnp.where(row == 0, high.astype(F32), jnp.where(row == 1, low.astype(F32), 0.0))
        for k, send in enumerate(send_refs):
            for start, width in tiles(features, 512):
                send[:tokens, start : start + width] = dot(
                    attended_ref[...], out_ref[k, :, start : start + width]
                ).astype(BF16)
            send[tokens : tokens + ROWS, :] = gains.astype(BF16)

    shapes = [struct((tokens, columns), BF16)]
    shapes += [struct((tokens + ROWS, features), BF16)] * (group - 1)
    return kernel_call(
        body,
        (query, *blocks, query_segments, out_slices, gain_row),
        tuple(shapes),
        flops=2 * tokens * columns * features * (group - 1),
        moved=2 * columns * features * (group - 1),
    )


def project_own(attended, out_slices):
    tokens, columns = attended.shape
    features = out_slices.shape[1]

    def body(attended_ref, out_ref, own_ref):
        for start, width in tiles(features, 512):
            own_ref[:, start : start + width] = dot(
                attended_ref[...], out_ref[:, start : start + width]
            ).astype(BF16)

    return kernel_call(
        body,
        (attended, out_slices),
        struct((tokens, features), BF16),
        flops=2 * tokens * columns * features,
        moved=2 * columns * features,
    )


def placement(picked, slots, devices, experts):
    tokens = picked.shape[1]
    expert = lax.broadcasted_iota(jnp.int32, (devices * experts, tokens), 0)
    chosen = expert == picked
    earlier = lax.broadcasted_iota(jnp.int32, (tokens, tokens), 0) < lax.broadcasted_iota(
        jnp.int32, (tokens, tokens), 1
    )
    before = dot(chosen.astype(F32).astype(BF16), earlier.astype(F32).astype(BF16))
    rank = jnp.sum(jnp.where(chosen, before, 0.0), axis=0, keepdims=True).astype(jnp.int32)
    target = lax.div(picked, jnp.full_like(picked, experts))
    local = picked - target * experts
    place = target * slots + local * CAPACITY + rank
    row = lax.broadcasted_iota(jnp.int32, (devices * slots, tokens), 0)
    return (row == place).astype(F32).astype(BF16)


def dispatch(own, received, residual_in, gain_row, modality, expert_in, slots, experts):
    devices = lax.axis_size("seq")
    tokens, features = own.shape
    count = len(received)

    def body(*refs):
        own_ref, received_refs = refs[0], refs[1 : 1 + count]
        residual_ref, gain_ref, modality_ref, expert_ref = refs[1 + count : 5 + count]
        total_ref, outgoing_ref = refs[5 + count :]
        picked = modality_ref[...] * MODAL_EXPERTS + expert_ref[...]
        places = placement(picked, slots, devices, experts)
        for start, width in tiles(features, 512):
            part = slice(start, start + width)
            attention = own_ref[:, part].astype(F32)
            for received_ref in received_refs:
                attention = attention + received_ref[:tokens, part].astype(F32)
            residual = residual_ref[:, part].astype(F32) + attention
            total_ref[:, part] = residual
            scaled = (residual * gain_ref[:, part]).astype(BF16)
            outgoing_ref[:, part] = dot(places, scaled).astype(BF16)

    return kernel_call(
        body,
        (own, *received, residual_in, gain_row, modality, expert_in),
        (struct((tokens, features), F32), struct((devices * slots, features), BF16)),
    )


def selection(expert, devices, slots, transpose):
    many, all_rows = devices * CAPACITY, devices * slots
    shape = (all_rows, many) if transpose else (many, all_rows)
    packed = lax.broadcasted_iota(jnp.int32, shape, 1 if transpose else 0)
    arrived = lax.broadcasted_iota(jnp.int32, shape, 0 if transpose else 1)
    shift = slots.bit_length() - 1
    source = arrived >> shift
    within = (arrived & (slots - 1)) - expert * CAPACITY
    hit = (within >= 0) & (within < CAPACITY) & (packed == source * CAPACITY + within)
    return hit.astype(F32).astype(BF16)


def take_rows(arrived_ref, rows_ref, expert, devices, slots):
    select = selection(expert, devices, slots, False)
    for start, width in tiles(rows_ref.shape[1], 512):
        part = slice(start, start + width)
        rows_ref[:, part] = dot(select, arrived_ref[:, part]).astype(BF16)


def row_statistics(rows_ref, gain, router_row):
    squares = logits = None
    for start, width in tiles(rows_ref.shape[1], 128):
        part = slice(start, start + width)
        row = rows_ref[:, part].astype(F32)
        plain = row * (1.0 / gain[:, part])
        product = row * router_row[:, part]
        squares = plain * plain if squares is None else squares + plain * plain
        logits = product if logits is None else logits + product
    return jnp.sum(squares, axis=1, keepdims=True), jnp.sum(logits, axis=1, keepdims=True)


def two_columns(first, second, rows):
    lane = lax.broadcasted_iota(jnp.int32, (rows, 128), 1)
    return jnp.where(lane == 0, first, jnp.where(lane == 1, second, 0.0))


def own_features(arrived, gate_slices, up_slices, gain_row, router_rows, slots):
    devices = lax.axis_size("seq")
    experts, features, hidden = gate_slices.shape
    many = devices * CAPACITY

    def body(arrived_ref, gate_ref, up_ref, gain_ref, router_ref, gates, ups, stats, rows_ref):
        me = lax.axis_index("exp")
        columns = pl.ds(pl.multiple_of(me * features, 128), features)
        for expert in range(experts):
            take_rows(arrived_ref, rows_ref, expert, devices, slots)
            router_row = router_ref[expert : expert + 1, columns].astype(F32)
            stats[expert] = two_columns(
                *row_statistics(rows_ref, gain_ref[...], router_row), many
            )
            for start, width in tiles(hidden, 256):
                part = slice(start, start + width)
                gates[expert, :, part] = dot(rows_ref[...], gate_ref[expert, :, part])
                ups[expert, :, part] = dot(rows_ref[...], up_ref[expert, :, part])

    return kernel_call(
        body,
        (arrived, gate_slices, up_slices, gain_row, router_rows),
        (
            pltpu.VMEM((experts, many, hidden), F32),
            pltpu.VMEM((experts, many, hidden), F32),
            pltpu.VMEM((experts, many, 128), F32),
        ),
        scratch=[pltpu.VMEM((many, features), BF16)],
        flops=4 * experts * many * features * hidden,
        moved=4 * experts * features * hidden,
        limit=8,
    )


def down_copies(down_ref, buffer, sems, target, features):
    experts, hidden, _ = down_ref.shape
    columns = pl.ds(pl.multiple_of(target * features, 128), features)
    copies = [
        pltpu.make_async_copy(down_ref.at[expert, :, columns], buffer.at[expert], sems.at[expert])
        for expert in range(experts)
    ]
    return copies


def expand_rows(hidden_ref, buffer, packed_ref, target_ref, devices, slots):
    experts, many, _ = hidden_ref.shape
    spread = [selection(expert, devices, slots, True) for expert in range(experts)]
    for start, width in tiles(target_ref.shape[1], 256):
        part = slice(start, start + width)
        laid = None
        for expert in range(experts):
            rows = dot(hidden_ref[expert], buffer[expert, :, part]).astype(BF16)
            placed = dot(spread[expert], rows)
            laid = placed if laid is None else laid + placed
        target_ref[:, part] = laid.astype(BF16)


def other_features(
    arrivals, gate_slices, up_slices, gains, router_rows, sums, down_weight, tokens, slots
):
    devices, group = lax.axis_size("seq"), lax.axis_size("exp")
    _, experts, features, hidden = gate_slices.shape
    many = devices * CAPACITY
    count = group - 1
    width_all = features * group

    def body(*refs):
        arrived_refs, refs = refs[:count], refs[count:]
        gain_refs, refs = refs[:count], refs[count:]
        gate_ref, up_ref, router_ref, gates, ups, stats, down_ref = refs[:7]
        hidden_ref, send_refs, refs = refs[7], refs[8 : 8 + count], refs[8 + count :]
        rows_ref, buffer, sems = refs
        me = lax.axis_index("exp")
        copies = [
            down_copies(
                down_ref, buffer.at[k], sems.at[k], lax.rem(me + k + 1, group), features
            )
            for k in range(count)
        ]
        for copy in [copy for some in copies for copy in some]:
            copy.start()
        for expert in range(experts):
            squares, logits = stats[expert][:, 0:1], stats[expert][:, 1:2]
            gate_sums = up_sums = None
            for k in range(count):
                behind = lax.rem(me + group - k - 1, group)
                columns = pl.ds(pl.multiple_of(behind * features, 128), features)
                take_rows(arrived_refs[k], rows_ref, expert, devices, slots)
                pair = gain_refs[k][tokens : tokens + ROWS, :].astype(F32)
                more_squares, more_logits = row_statistics(
                    rows_ref,
                    pair[0:1, :] + pair[1:2, :],
                    router_ref[expert : expert + 1, columns].astype(F32),
                )
                squares, logits = squares + more_squares, logits + more_logits
                if k < count - 1:
                    for start, width in tiles(hidden, 256):
                        part = slice(start, start + width)
                        gates[expert, :, part] += dot(
                            rows_ref[...], gate_ref[k, expert, :, part]
                        )
                        ups[expert, :, part] += dot(rows_ref[...], up_ref[k, expert, :, part])
            scale = lax.rsqrt(squares / width_all + EPSILON)
            router_gate = 1.0 / (1.0 + jnp.exp(-(logits * scale)))
            for start, width in tiles(hidden, 256):
                part = slice(start, start + width)
                gate = gates[expert, :, part] + dot(
                    rows_ref[...], gate_ref[count - 1, expert, :, part]
                )
                up = ups[expert, :, part] + dot(rows_ref[...], up_ref[count - 1, expert, :, part])
                gate, up = gate * scale, up * scale
                hidden_ref[expert, :, part] = (
                    gate / (1.0 + jnp.exp(-gate)) * up * router_gate
                ).astype(BF16)
        for k in range(count):
            for copy in copies[k]:
                copy.wait()
            expand_rows(hidden_ref, buffer.at[k], None, send_refs[k], devices, slots)

    shapes = [struct((experts, many, hidden), BF16)]
    shapes += [struct((devices * slots, features), BF16)] * count
    ins = (*arrivals, *gains, gate_slices, up_slices, router_rows, *sums, down_weight)
    return kernel_call(
        body,
        ins,
        tuple(shapes),
        specs=[VMEM] * (len(ins) - 1) + [ANY],
        scratch=[
            pltpu.VMEM((many, features), BF16),
            pltpu.VMEM((count, experts, hidden, features), BF16),
            pltpu.SemaphoreType.DMA((count, experts)),
        ],
        flops=6 * experts * many * features * hidden,
        moved=2 * experts * features * hidden,
        limit=22,
    )


def own_outputs(hidden_rows, down_weight, features, slots):
    devices = lax.axis_size("seq")
    experts, many, hidden = hidden_rows.shape

    def body(hidden_ref, down_ref, own_ref, buffer, sems):
        copies = down_copies(down_ref, buffer, sems, lax.axis_index("exp"), features)
        for copy in copies:
            copy.start()
        for copy in copies:
            copy.wait()
        expand_rows(hidden_ref, buffer, None, own_ref, devices, slots)

    return kernel_call(
        body,
        (hidden_rows, down_weight),
        struct((devices * slots, features), BF16),
        specs=[VMEM, ANY],
        scratch=[
            pltpu.VMEM((experts, hidden, features), BF16),
            pltpu.SemaphoreType.DMA((experts,)),
        ],
        flops=2 * experts * many * features * hidden,
        moved=2 * experts * features * hidden,
    )


def add_groups(own, received):
    def body(*refs):
        total = refs[0][...].astype(F32)
        for ref in refs[1:-1]:
            total = total + ref[...].astype(F32)
        refs[-1][...] = total.astype(BF16)

    return kernel_call(body, (own, *received), struct(own.shape, BF16))


def finish(residual, returned, modality, expert_in, slots, experts):
    devices = lax.axis_size("seq")
    tokens, features = residual.shape

    def body(residual_ref, returned_ref, modality_ref, expert_ref, out_ref):
        picked = modality_ref[...] * MODAL_EXPERTS + expert_ref[...]
        places = placement(picked, slots, devices, experts)
        for start, width in tiles(features, 512):
            part = slice(start, start + width)
            routed = dot(places, returned_ref[:, part], ((0,), (0,)))
            out_ref[:, part] = (residual_ref[:, part] + routed).astype(BF16)

    return kernel_call(
        body,
        (residual, returned, modality, expert_in),
        struct((tokens, features), BF16),
    )


def local(
    query_input,
    key_input,
    value_input,
    segment_ids,
    residual_in,
    out_weight,
    norm_gain,
    router,
    modality,
    expert_in,
    gate_weight,
    up_weight,
    down_weight,
):
    tokens, columns = query_input.shape
    features = residual_in.shape[1]
    devices, group = lax.axis_size("seq"), lax.axis_size("exp")
    experts = gate_weight.shape[0]
    slots = max(ROWS, 1 << (experts * CAPACITY - 1).bit_length())
    marks = segment_ids + 1
    gain_row = norm_gain.reshape(1, features)
    router_rows = router.T
    modality, expert_in = modality.reshape(1, tokens), expert_in.reshape(1, tokens)
    mark_rows = jnp.broadcast_to(
        jnp.tile(marks.astype(BF16), columns // tokens)[None, :], (ROWS, columns)
    )
    packed = jnp.concatenate([key_input, value_input, mark_rows], axis=0)
    blocks = [shifted(packed, "seq", step) for step in range(1, devices // 8 + 1)]
    out_own, gate_own, up_own, out_others, gate_others, up_others = [
        pltpu.with_memory_space_constraint(value, pltpu.VMEM)
        for value in fetch_weights(out_weight, gate_weight, up_weight, features)
    ]
    attended, *contributions = attend(
        query_input,
        [packed, *blocks],
        marks.astype(F32).reshape(tokens, 1),
        out_others,
        gain_row,
    )
    received = [rotated(value, "exp", k + 1) for k, value in enumerate(contributions)]
    own = project_own(attended, out_own)
    residual, outgoing = dispatch(
        own, received, residual_in, gain_row, modality, expert_in, slots, experts
    )

    def exchanged(value):
        value = value.reshape(devices, slots, features)
        value = lax.all_to_all(value, "seq", split_axis=0, concat_axis=0, tiled=True)
        return value.reshape(devices * slots, features)

    arrived = exchanged(outgoing)
    arrivals = [rotated(arrived, "exp", k) for k in range(1, group)]
    sums = own_features(arrived, gate_own, up_own, gain_row, router_rows, slots)
    hidden_rows, *partials = other_features(
        arrivals,
        gate_others,
        up_others,
        received,
        router_rows,
        sums,
        down_weight,
        tokens,
        slots,
    )
    others = [rotated(value, "exp", k + 1) for k, value in enumerate(partials)]
    own_part = own_outputs(hidden_rows, down_weight, features, slots)
    returned = exchanged(add_groups(own_part, others))
    return finish(residual, returned, modality, expert_in, slots, experts)


def solution(mesh):
    in_specs = (
        P("seq", "exp"),
        P("seq", "exp"),
        P("seq", "exp"),
        P("seq"),
        P("seq", "exp"),
        P("exp", None),
        P("exp"),
        P(None, "seq"),
        P("seq"),
        P("seq"),
        P("seq", None, "exp"),
        P("seq", None, "exp"),
        P("seq", "exp", None),
    )
    return jax.shard_map(
        local, mesh=mesh, in_specs=in_specs, out_specs=P("seq", "exp"), check_vma=False
    )
```

time: 197 us -> 157 us (0.80)
  waiting for transfers between devices: 60.4 us -> 1.25 us
  Pallas kernels: 0 us -> 47 us
  matrix products: 38.4 us -> 0 us
  blocking collectives: 35.7 us -> 62.5 us
  local copies, waits for them, and re-layouts: 10.8 us -> 35.3 us
  starting transfers between devices: 29.9 us -> 8.98 us
  between operations: 13.4 us -> 0.21 us
  other arithmetic: 7.13 us -> 1.72 us
    pallas_call x0 -> x9, Pallas kernels: none -> 47 us  [kernel_call(): pl.pallas_call(body, in_specs=specs, out_specs=outs, out_shape=out_shape,...]
    dot_general x10 -> x0, matrix products: 38.4 us -> none  [the longest x1 18.9 us: local(): jnp.einsum('erf,efd->erd', hidden, down_weight, preferred_element_type=jn...]
    unnamed x25 -> x34, local copies, waits for them, and re-layouts: 2.74 us -> 35.2 us
    all_to_all x1 -> x2, blocking collectives: 33.3 us -> 62.5 us  [exchanged(): lax.all_to_all(value, 'seq', split_axis=0, concat_axis=0, tiled=True)]
    all_to_all x1 -> x0, waiting for transfers between devices: 22.4 us -> none  [local(): lax.all_to_all(summed, 'seq', split_axis=1, concat_axis=0, tiled=True)]
    reduce_scatter x2 -> x0, waiting for transfers between devices: 21.8 us -> none  [the longest x1 11.2 us: local(): lax.psum_scatter(projected.astype(jnp.bfloat16), 'exp', scatter_dimension...]
    ppermute x6 -> x5, starting transfers between devices: 22.9 us -> 8.98 us  [the longest x2 8.34 us: shifted(): lax.ppermute(value, axis, [(source, source + steps) for source in range(l...]
    all_gather x1 -> x0, waiting for transfers between devices: 8.56 us -> none  [local(): arrived = lax.all_gather(sliced, 'exp', axis=2, tiled=True)]
  transfers between devices with their start and end apart: 10 -> 5, of which waited for: 6 -> 1; matrix products, arithmetic and copies ran while one was open for 1% -> 0% of each run, Pallas kernels for 0% -> 18%
where the time goes in v1:
time: 157 us
  blocking collectives  62.5 us (40%)
  Pallas kernels  47 us (30%)
  local copies, waits for them, and re-layouts  35.3 us (22%)
  starting transfers between devices  8.98 us (6%)
  other arithmetic  1.72 us (1%)
    all_to_all x2, blocking collectives, exchanged(): lax.all_to_all(value, 'seq', split_axis=0, concat_axis=0, tiled=True)  62.5 us
    pallas_call x9, Pallas kernels, kernel_call(): pl.pallas_call(body, in_specs=specs, out_specs=outs, out_shape=out_shape,...  47 us
    unnamed x34, local copies, waits for them, and re-layouts  35.2 us
    ppermute x2, starting transfers between devices, shifted(): lax.ppermute(value, axis, [(source, source + steps) for source in range(l...  8.34 us
  transfers between devices with their start and end apart: 5, of which 1 were waited for; matrix products, arithmetic and copies ran while one was open for 0% of the time, Pallas kernels for 18%

profile of v1, /device:TPU:0, one launch (start us, length us, event | category | flops | bytes accessed | tf_op | source)
XLA Modules:
  0.0 156.9 jit_solution(11297230561750492779)
XLA Ops:
  0.0 0.7 convert_bitcast_fusion
  0.7 1.1 pad_maximum_fusion.refs_1_
  1.7 4.9 %collective-permute-start.1 = (bf16[272,1024]{1,0:T(8,128)(2,1)S(1)}, bf16[272,1024]{1,0:T(8,128)(2,1)S(1)}, u32[]{:S(2)}, u32[]{:S(2)}) collective-permute-start(bf16[272,1024]{1,0:T(8,128)(2,1)S(1)} %pad_maximum_fusion.refs_1_), channel_id=1, source_target_pairs={{0,4},{2,6},{4,8},{6,10},{8,12},{10,14},{12,16},{14,18},{16,20},{1... | collective-permute-start | bytes 1671176 | tf_op jit(solution)/shard_map/ppermute | solution.py:36
  6.7 3.4 %collective-permute-start = (bf16[272,1024]{1,0:T(8,128)(2,1)S(1)}, bf16[272,1024]{1,0:T(8,128)(2,1)S(1)}, u32[]{:S(2)}, u32[]{:S(2)}) collective-permute-start(bf16[272,1024]{1,0:T(8,128)(2,1)S(1)} %pad_maximum_fusion.refs_1_), channel_id=1, source_target_pairs={{0,2},{2,4},{4,6},{6,8},{8,10},{10,12},{12,14},{14,16},{16,18},{18... | collective-permute-start | bytes 1671176 | tf_op jit(solution)/shard_map/ppermute | solution.py:36
  10.1 0.1 copy.14.refs_4_
  10.2 0.0 copy-start.13
  10.2 16.7 %shard_map.127 = (bf16[1024,2048]{1,0:T(8,128)(2,1)S(1)}, bf16[2,2048,1408]{2,1,0:T(8,128)(2,1)S(1)}, bf16[2,2048,1408]{2,1,0:T(8,128)(2,1)S(1)}, bf16[1,1024,20...) custom-call(bf16[1024,4096]{1,0:T(8,128)(2,1)} %refs_0_.2, ...), custom_call_target="tpu_custom_call" | custom-call | bytes 54525952 | tf_op jit(solution)/shard_map/pallas_call | solution.py:51
  26.9 4.2 %copy-done.1 = bf16[2,2048,1408]{2,1,0:T(8,128)(2,1)} copy-done((bf16[2,2048,1408]{2,1,0:T(8,128)(2,1)}, bf16[2,2048,1408]{2,1,0:T(8,128)(2,1)S(1)}, u32[]{:S(2)}) %copy-start.1) | copy-done | bytes 11534360
  31.1 4.1 %copy-done.3 = bf16[2,2048,1408]{2,1,0:T(8,128)(2,1)} copy-done((bf16[2,2048,1408]{2,1,0:T(8,128)(2,1)}, bf16[2,2048,1408]{2,1,0:T(8,128)(2,1)S(1)}, u32[]{:S(2)}) %copy-start.3) | copy-done | bytes 11534360
  35.3 4.3 %copy-done.5 = bf16[1,2,2048,1408]{3,2,1,0:T(8,128)(2,1)} copy-done((bf16[1,2,2048,1408]{3,2,1,0:T(8,128)(2,1)}, bf16[1,2,2048,1408]{3,2,1,0:T(8,128)(2,1)S(1)}, u32[]{:S(2)}) %copy-start.5) | copy-done | bytes 11534360
  39.6 4.2 %copy-done.7 = bf16[1,2,2048,1408]{3,2,1,0:T(8,128)(2,1)} copy-done((bf16[1,2,2048,1408]{3,2,1,0:T(8,128)(2,1)}, bf16[1,2,2048,1408]{3,2,1,0:T(8,128)(2,1)S(1)}, u32[]{:S(2)}) %copy-start.7) | copy-done | bytes 11534360
  43.8 0.0 copy-start.15
  43.8 0.0 copy-start.16
  43.9 3.1 %shard_map.128 = (bf16[128,1024]{1,0:T(8,128)(2,1)S(1)}, bf16[144,2048]{1,0:T(8,128)(2,1)S(1)}) custom-call(bf16[128,1024]{1,0:T(8,128)(2,1)S(1)} %copy-done.12, bf16[272,1024]{1,0:T(8,128)(2,1)S(1)} %pad_maximum_fusion.refs_1_, bf16[272,1024]{1,0:T(8,128)(2,1)S(1)} %collective-permute-done.refs_2_, bf16[272,1024]{1,0:T(8,128)(2,1)S(1)} %collective-permute-done.1.refs_3_, ...), custom_call_target="tpu_custom_call" | custom-call | flops 536870912 | bytes 4194304 | tf_op jit(solution)/shard_map/pallas_call | solution.py:51
  46.9 0.1 collective-permute-start.2
  47.0 0.0 copy-start.14
  47.0 0.7 shard_map.129.refs_0_
  47.8 1.2 collective-permute-done.2.refs_1_
  49.0 0.6 shard_map.130
  49.6 32.2 %all_to_all.10 = bf16[16,16,2048]{2,1,0:T(8,128)(2,1)S(1)} all-to-all(bf16[16,16,2048]{2,1,0:T(8,128)(2,1)S(1)} %bitcast.16), channel_id=1, replica_groups=mesh['seq'=16,'exp'=2] {'seq'}, dimensions={0} | all-to-all | bytes 2097152 | tf_op jit(solution)/shard_map/all_to_all | solution.py:517
  81.8 4.3 %copy-done.4 = bf16[2,2048,1408]{2,1,0:T(8,128)(2,1)S(1)} copy-done((bf16[2,2048,1408]{2,1,0:T(8,128)(2,1)S(1)}, bf16[2,2048,1408]{2,1,0:T(8,128)(2,1)}, u32[]{:S(2)}) %copy-start.4) | copy-done | bytes 11534360
  86.1 4.5 %shard_map.131 = (f32[2,112,1408]{2,1,0:T(8,128)S(1)}, f32[2,112,1408]{2,1,0:T(8,128)S(1)}, f32[2,112,128]{2,1,0:T(8,128)S(1)}) custom-call(bf16[256,2048]{1,0:T(8,128)(2,1)S(1)} %bitcast.13, bf16[2,2048,1408]{2,1,0:T(8,128)(2,1)S(1)} %copy-done.2, bf16[2,2048,1408]{2,1,0:T(8,128)(2,1)S(1)} %copy-done.4, f32[1,2048]{1,0:T(1,128)S(1)} %bitcast.19, ...), custom_call_target="tpu_custom_call" | custom-call | flops 2583691264 | bytes 23068672 | tf_op jit(solution)/shard_map/pallas_call | solution.py:51
  90.7 1.0 copy-done.9
  91.6 4.3 %copy-done.8 = bf16[1,2,2048,1408]{3,2,1,0:T(8,128)(2,1)S(1)} copy-done((bf16[1,2,2048,1408]{3,2,1,0:T(8,128)(2,1)S(1)}, bf16[1,2,2048,1408]{3,2,1,0:T(8,128)(2,1)}, u32[]{:S(2)}) %copy-start.8) | copy-done | bytes 11534360
  95.9 1.2 copy-done.10
  97.1 12.9 %shard_map.132 = (bf16[2,112,1408]{2,1,0:T(8,128)(2,1)S(1)}, bf16[256,2048]{1,0:T(8,128)(2,1)S(1)}) custom-call(bf16[256,2048]{1,0:T(8,128)(2,1)S(1)} %copy-done.10, bf16[144,2048]{1,0:T(8,128)(2,1)S(1)} %collective-permute-done.2.refs_1_, bf16[1,2,2048,1408]{3,2,1,0:T(8,128)(2,1)S(1)} %copy-done.6, bf16[1,2,2048,1408]{3,2,1,0:T(8,128)(2,1)S(1)} %copy-done.8, ...), custom_call_target="tpu_custom_call" | custom-call | flops 3875536896 | bytes 11534336 | tf_op jit(solution)/shard_map/pallas_call | solution.py:51
  110.0 0.6 collective-permute-start.4
  110.6 7.6 %copy-done = bf16[2,1408,4096]{2,1,0:T(8,128)(2,1)S(1)} copy-done((bf16[2,1408,4096]{2,1,0:T(8,128)(2,1)S(1)}, bf16[2,1408,4096]{2,1,0:T(8,128)(2,1)}, u32[]{:S(2)}) %copy-start) | copy-done | bytes 23068696
  118.2 6.9 %shard_map.133.refs_0_ = bf16[256,2048]{1,0:T(8,128)(2,1)S(1)} custom-call(bf16[2,112,1408]{2,1,0:T(8,128)(2,1)S(1)} %get-tuple-element.33.hidden_ref, bf16[2,1408,4096]{2,1,0:T(8,128)(2,1)S(1)} %copy-done), custom_call_target="tpu_custom_call" | custom-call | flops 1291845632 | bytes 11534336 | tf_op jit(solution)/shard_map/pallas_call | solution.py:51
  125.1 0.2 shard_map.134
  125.4 30.3 %all_to_all.11 = bf16[16,16,2048]{2,1,0:T(8,128)(2,1)S(1)} all-to-all(bf16[16,16,2048]{2,1,0:T(8,128)(2,1)S(1)} %bitcast.15), channel_id=1, replica_groups=mesh['seq'=16,'exp'=2] {'seq'}, dimensions={0} | all-to-all | bytes 2097152 | tf_op jit(solution)/shard_map/all_to_all | solution.py:517
  155.7 1.3 shard_map.135
  (28 shorter events, 0.1 us)
Async XLA Ops:
  1.7 42.0 %collective-permute-start.1 = (bf16[272,1024]{1,0:T(8,128)(2,1)S(1)}, bf16[272,1024]{1,0:T(8,128)(2,1)S(1)}, u32[]{:S(2)}, u32[]{:S(2)}) collective-permute-start(bf16[272,1024]{1,0:T(8,128)(2,1)S(1)} %pad_maximum_fusion.refs_1_), channel_id=1, source_target_pairs={{0,4},{2,6},{4,8},{6,10},{8,12},{10,14},{12,16},{14,18},{16,20},{1... | collective-permute-start | bytes 1671176 | tf_op jit(solution)/shard_map/ppermute | solution.py:36
  6.7 37.1 %collective-permute-start = (bf16[272,1024]{1,0:T(8,128)(2,1)S(1)}, bf16[272,1024]{1,0:T(8,128)(2,1)S(1)}, u32[]{:S(2)}, u32[]{:S(2)}) collective-permute-start(bf16[272,1024]{1,0:T(8,128)(2,1)S(1)} %pad_maximum_fusion.refs_1_), channel_id=1, source_target_pairs={{0,2},{2,4},{4,6},{6,8},{8,10},{10,12},{12,14},{14,16},{16,18},{18... | collective-permute-start | bytes 1671176 | tf_op jit(solution)/shard_map/ppermute | solution.py:36
  10.2 33.6 %copy-start.12 = (bf16[128,1024]{1,0:T(8,128)(2,1)S(1)}, bf16[128,1024]{1,0:T(8,128)(2,1)}, u32[]{:S(2)}) copy-start(bf16[128,1024]{1,0:T(8,128)(2,1)} %refs_0_.3) | copy-start | bytes 786436
  10.2 33.6 %copy-start.13 = (f32[2048]{0:T(1024)S(1)}, f32[2048]{0:T(1024)}, u32[]{:S(2)}) copy-start(f32[2048]{0:T(1024)} %param.19) | copy-start | bytes 24580
  26.9 4.2 %copy-start.1 = (bf16[2,2048,1408]{2,1,0:T(8,128)(2,1)}, bf16[2,2048,1408]{2,1,0:T(8,128)(2,1)S(1)}, u32[]{:S(2)}) copy-start(bf16[2,2048,1408]{2,1,0:T(8,128)(2,1)S(1)} %get-tuple-element.28.gate_ref) | copy-start | bytes 34603012
  31.1 4.1 %copy-start.3 = (bf16[2,2048,1408]{2,1,0:T(8,128)(2,1)}, bf16[2,2048,1408]{2,1,0:T(8,128)(2,1)S(1)}, u32[]{:S(2)}) copy-start(bf16[2,2048,1408]{2,1,0:T(8,128)(2,1)S(1)} %get-tuple-element.29.up_ref) | copy-start | bytes 34603012
  35.3 4.3 %copy-start.5 = (bf16[1,2,2048,1408]{3,2,1,0:T(8,128)(2,1)}, bf16[1,2,2048,1408]{3,2,1,0:T(8,128)(2,1)S(1)}, u32[]{:S(2)}) copy-start(bf16[1,2,2048,1408]{3,2,1,0:T(8,128)(2,1)S(1)} %get-tuple-element.26.refs_2_) | copy-start | bytes 34603012
  39.6 4.2 %copy-start.7 = (bf16[1,2,2048,1408]{3,2,1,0:T(8,128)(2,1)}, bf16[1,2,2048,1408]{3,2,1,0:T(8,128)(2,1)S(1)}, u32[]{:S(2)}) copy-start(bf16[1,2,2048,1408]{3,2,1,0:T(8,128)(2,1)S(1)} %get-tuple-element.27.refs_3_) | copy-start | bytes 34603012
  43.8 5.2 %copy-start.11 = (bf16[128,2048]{1,0:T(8,128)(2,1)S(1)}, bf16[128,2048]{1,0:T(8,128)(2,1)}, u32[]{:S(2)}) copy-start(bf16[128,2048]{1,0:T(8,128)(2,1)} %refs_2_.3) | copy-start | bytes 1572868
  43.8 5.2 %copy-start.15 = (s32[128]{0:T(128)S(1)}, s32[128]{0:T(128)}, u32[]{:S(2)}) copy-start(s32[128]{0:T(128)} %param.21) | copy-start | bytes 1540
  43.8 5.2 %copy-start.16 = (s32[128]{0:T(128)S(1)}, s32[128]{0:T(128)}, u32[]{:S(2)}) copy-start(s32[128]{0:T(128)} %param.22) | copy-start | bytes 1540
  43.8 38.0 %copy-start.2 = (bf16[2,2048,1408]{2,1,0:T(8,128)(2,1)S(1)}, bf16[2,2048,1408]{2,1,0:T(8,128)(2,1)}, u32[]{:S(2)}) copy-start(bf16[2,2048,1408]{2,1,0:T(8,128)(2,1)} %copy-done.1) | copy-start | bytes 34603012
  46.9 2.1 %collective-permute-start.2 = (bf16[144,2048]{1,0:T(8,128)(2,1)S(1)}, bf16[144,2048]{1,0:T(8,128)(2,1)S(1)}, u32[]{:S(2)}, u32[]{:S(2)}) collective-permute-start(bf16[144,2048]{1,0:T(8,128)(2,1)S(1)} %get-tuple-element.23), channel_id=1, source_target_pairs={{0,1},{1,0},{2,3},{3,2},{4,5},{5,4},{6,7},{7,6},{8,9},{9,8},{10,11... | collective-permute-start | bytes 1769480 | tf_op jit(solution)/shard_map/ppermute | solution.py:41
  47.0 34.8 %copy-start.14 = (bf16[4096,2]{0,1:T(2,128)(2,1)S(1)}, bf16[4096,2]{0,1:T(2,128)(2,1)}, u32[]{:S(2)}) copy-start(bf16[4096,2]{0,1:T(2,128)(2,1)} %param.20) | copy-start | bytes 49156
  81.8 8.8 %collective-permute-start.3 = (bf16[256,2048]{1,0:T(8,128)(2,1)S(1)}, bf16[256,2048]{1,0:T(8,128)(2,1)S(1)}, u32[]{:S(2)}, u32[]{:S(2)}) collective-permute-start(bf16[256,2048]{1,0:T(8,128)(2,1)S(1)} %bitcast.12), channel_id=1, source_target_pairs={{0,1},{1,0},{2,3},{3,2},{4,5},{5,4},{6,7},{7,6},{8,9},{9,8},{10,11... | collective-permute-start | bytes 3145736 | tf_op jit(solution)/shard_map/ppermute | solution.py:41
  81.8 4.3 %copy-start.4 = (bf16[2,2048,1408]{2,1,0:T(8,128)(2,1)S(1)}, bf16[2,2048,1408]{2,1,0:T(8,128)(2,1)}, u32[]{:S(2)}) copy-start(bf16[2,2048,1408]{2,1,0:T(8,128)(2,1)} %copy-done.3) | copy-start | bytes 34603012
  86.1 5.5 %copy-start.6 = (bf16[1,2,2048,1408]{3,2,1,0:T(8,128)(2,1)S(1)}, bf16[1,2,2048,1408]{3,2,1,0:T(8,128)(2,1)}, u32[]{:S(2)}) copy-start(bf16[1,2,2048,1408]{3,2,1,0:T(8,128)(2,1)} %copy-done.5) | copy-start | bytes 34603012
  90.7 1.0 copy-start.9
  91.6 4.3 %copy-start.8 = (bf16[1,2,2048,1408]{3,2,1,0:T(8,128)(2,1)S(1)}, bf16[1,2,2048,1408]{3,2,1,0:T(8,128)(2,1)}, u32[]{:S(2)}) copy-start(bf16[1,2,2048,1408]{3,2,1,0:T(8,128)(2,1)} %copy-done.7) | copy-start | bytes 34603012
  95.9 1.2 copy-start.10
  110.0 15.1 %collective-permute-start.4 = (bf16[256,2048]{1,0:T(8,128)(2,1)S(1)}, bf16[256,2048]{1,0:T(8,128)(2,1)S(1)}, u32[]{:S(2)}, u32[]{:S(2)}) collective-permute-start(bf16[256,2048]{1,0:T(8,128)(2,1)S(1)} %get-tuple-element.34), channel_id=1, source_target_pairs={{0,1},{1,0},{2,3},{3,2},{4,5},{5,4},{6,7},{7,6},{8,9},{9,8},{10,11... | collective-permute-start | bytes 3145736 | tf_op jit(solution)/shard_map/ppermute | solution.py:41
  110.6 7.6 %copy-start = (bf16[2,1408,4096]{2,1,0:T(8,128)(2,1)S(1)}, bf16[2,1408,4096]{2,1,0:T(8,128)(2,1)}, u32[]{:S(2)}) copy-start(bf16[2,1408,4096]{2,1,0:T(8,128)(2,1)} %down_ref.1) | copy-start | bytes 69206016

commit v2 on v1

v2 whole, which is shorter than its diff:
```python
import functools

import jax
import jax.numpy as jnp
from jax import lax
from jax.experimental import pallas as pl
from jax.experimental.pallas import tpu as pltpu
from jax.sharding import PartitionSpec as P

HEAD_DIM = 128
MODAL_EXPERTS = 16
CAPACITY = 7
NEGATIVE = -1e30
EPSILON = 1e-05
ROWS = 16
MIB = 1 << 20

F32 = jnp.float32
BF16 = jnp.bfloat16

ANY = pl.BlockSpec(memory_space=pl.ANY)
VMEM = pl.BlockSpec(memory_space=pltpu.VMEM)


def tiles(width, size):
    return [(start, min(size, width - start)) for start in range(0, width, size)]


def dot(left, right, dims=((1,), (0,))):
    return lax.dot_general(left, right, (dims, ((), ())), preferred_element_type=F32)


def shifted(value, axis, steps):
    count = lax.axis_size(axis)
    leading, last = max(0, -steps), min(count, count - steps)
    return lax.ppermute(value, axis, [(source, source + steps) for source in range(leading, last)])


def rotated(value, axis, steps):
    count = lax.axis_size(axis)
    return lax.ppermute(value, axis, [(source, (source + steps) % count) for source in range(count)])


def cost(flops, moved):
    return pl.CostEstimate(flops=int(flops), bytes_accessed=int(moved), transcendentals=0)


def kernel_call(body, ins, out_shape, specs=None, scratch=(), flops=0, moved=0, limit=16):
    specs = specs or [VMEM] * len(ins)
    outs = jax.tree.map(lambda _: VMEM, out_shape)
    return pl.pallas_call(
        body,
        in_specs=specs,
        out_specs=outs,
        out_shape=out_shape,
        scratch_shapes=list(scratch),
        cost_estimate=cost(flops, moved),
        compiler_params=pltpu.CompilerParams(vmem_limit_bytes=limit * MIB),
    )(*ins)


def struct(shape, dtype):
    return jax.ShapeDtypeStruct(shape, dtype)


def pack_keys(key_input, value_input, segment_row):
    tokens, columns = key_input.shape

    def body(key_ref, value_ref, segment_ref, packed_ref, row_ref, sems):
        pairs = (
            (segment_ref, row_ref),
            (key_ref, packed_ref.at[:tokens, :]),
            (value_ref, packed_ref.at[tokens : 2 * tokens, :]),
        )
        copies = [
            pltpu.make_async_copy(source, target, sems.at[index])
            for index, (source, target) in enumerate(pairs)
        ]
        for copy in copies:
            copy.start()
        copies[0].wait()
        marks = jnp.broadcast_to((row_ref[...] + 1).astype(F32), (ROWS, tokens)).astype(BF16)
        for start in range(0, columns, tokens):
            packed_ref[2 * tokens : 2 * tokens + ROWS, start : start + tokens] = marks
        for copy in copies[1:]:
            copy.wait()

    return kernel_call(
        body,
        [
            pltpu.with_memory_space_constraint(value, pltpu.HBM)
            for value in (key_input, value_input, segment_row)
        ],
        pltpu.VMEM((2 * tokens + ROWS, columns), BF16),
        specs=[ANY] * 3,
        scratch=[pltpu.VMEM((1, tokens), jnp.int32), pltpu.SemaphoreType.DMA((3,))],
        limit=4,
    )


def prepare(out_weight, gate_weight, up_weight, modality, expert_in, feature_count, layout):
    devices, group = lax.axis_size("seq"), lax.axis_size("exp")
    head_rows = out_weight.shape[0]
    experts, _, hidden = gate_weight.shape
    rows, _, spare, tile_count, _ = layout
    tokens = modality.shape[1]
    kinds = 2 if spare else 1
    many = devices * CAPACITY

    def body(*refs):
        out_ref, gate_ref, up_ref, modality_ref, expert_ref = refs[:5]
        out_own, out_others, places_ref, take_ref, spread_ref = refs[5:10]
        slices, sems = refs[10:-1], refs[-1]
        me = lax.axis_index("exp")
        copies = []
        for k in range(group):
            ahead = lax.rem(me + k, group)
            columns = pl.ds(pl.multiple_of(ahead * feature_count, 128), feature_count)
            copies.append((out_ref.at[:, columns], out_others.at[k - 1] if k else out_own))
        wanted = [(up_ref, 0)] + [(gate_ref, k) for k in range(group)]
        for which, (ref, k) in enumerate(wanted):
            behind = lax.rem(me + group - k, group)
            part = pl.ds(pl.multiple_of(behind * feature_count, 128), feature_count)
            for expert in range(experts):
                copies.append((ref.at[expert, part, :], slices[which * experts + expert]))
        started = [
            pltpu.make_async_copy(source, target, sems.at[index])
            for index, (source, target) in enumerate(copies)
        ]
        for copy in started:
            copy.start()
        picked = modality_ref[...] * MODAL_EXPERTS + expert_ref[...]
        main, last = placement(picked, layout, devices, experts)
        places_ref[0] = main
        for tile, value in enumerate(last):
            places_ref[1 + tile] = value
        for tile in range(tile_count):
            for kind in range(kinds):
                which = tile if kind else None
                for expert in range(experts):
                    start = (kind * experts + expert) * many
                    take_ref[tile, start : start + many, :] = selection(
                        expert, layout, devices, which
                    )
                spread_ref[tile, :, kind * experts * many : (kind + 1) * experts * many] = (
                    spreading(layout, experts, devices, which)
                )
        for copy in started:
            copy.wait()

    shapes = (
        pltpu.VMEM((head_rows, feature_count), BF16),
        pltpu.VMEM((group - 1, head_rows, feature_count), BF16),
        pltpu.VMEM((1 + (tile_count if spare else 0), devices * rows, tokens), BF16),
        pltpu.VMEM((tile_count, kinds * experts * many, devices * rows), BF16),
        pltpu.VMEM((tile_count, devices * rows, kinds * experts * many), BF16),
        *[pltpu.VMEM((feature_count, hidden), BF16)] * ((1 + group) * experts),
    )
    return kernel_call(
        body,
        (out_weight, gate_weight, up_weight, modality, expert_in),
        shapes,
        specs=[ANY] * 3 + [VMEM] * 2,
        scratch=[pltpu.SemaphoreType.DMA((group + (1 + group) * experts,))],
        moved=2 * (out_weight.size + gate_weight.size + up_weight.size),
        limit=4,
    )


def attend(query, blocks, out_slices, gain_row):
    group = lax.axis_size("exp")
    tokens, columns = query.shape
    features = out_slices.shape[2]
    count = len(blocks)

    def body(*refs):
        query_ref, block_refs = refs[0], refs[1 : 1 + count]
        out_ref, gain_ref = refs[1 + count : 3 + count]
        attended_ref, send_refs = refs[3 + count], refs[4 + count :]
        key_pos = lax.broadcasted_iota(jnp.int32, (tokens, tokens), 1)
        query_pos = lax.broadcasted_iota(jnp.int32, (tokens, tokens), 0)
        marks = block_refs[0][2 * tokens : 2 * tokens + ROWS, :tokens]
        own = dot(one_hot(key_pos == query_pos), marks, ((1,), (1,)))[:, 0:1]
        masks = []
        for index, block in enumerate(block_refs):
            theirs = block[2 * tokens : 2 * tokens + ROWS, :tokens].astype(F32)[0:1, :]
            mask = jnp.broadcast_to(own, (tokens, tokens)) == jnp.broadcast_to(
                theirs, (tokens, tokens)
            )
            if index == 0:
                mask = mask & (key_pos <= query_pos)
            masks.append(mask)
        for head in range(columns // HEAD_DIM):
            part = slice(head * HEAD_DIM, (head + 1) * HEAD_DIM)
            heads = query_ref[:, part]
            scores = [
                jnp.where(
                    mask,
                    dot(heads, block[:tokens, part], ((1,), (1,))) * HEAD_DIM ** (-0.5),
                    NEGATIVE,
                )
                for block, mask in zip(block_refs, masks)
            ]
            peak = functools.reduce(
                jnp.maximum, [jnp.max(score, axis=1, keepdims=True) for score in scores]
            )
            weights = [jnp.exp(score - peak) for score in scores]
            total = sum(jnp.sum(weight, axis=1, keepdims=True) for weight in weights)
            summed = sum(
                dot(weight.astype(BF16), block[tokens : 2 * tokens, part])
                for weight, block in zip(weights, block_refs)
            )
            attended_ref[:, part] = (summed / total).astype(BF16)
        high = gain_ref[...].astype(BF16)
        low = (gain_ref[...] - high.astype(F32)).astype(BF16)
        row = lax.broadcasted_iota(jnp.int32, (ROWS, features), 0)
        gains = jnp.where(row == 0, high.astype(F32), jnp.where(row == 1, low.astype(F32), 0.0))
        for k, send in enumerate(send_refs):
            for start, width in tiles(features, 512):
                send[:tokens, start : start + width] = dot(
                    attended_ref[...], out_ref[k, :, start : start + width]
                ).astype(BF16)
            send[tokens : tokens + ROWS, :] = gains.astype(BF16)

    shapes = [struct((tokens, columns), BF16)]
    shapes += [struct((tokens + ROWS, features), BF16)] * (group - 1)
    return kernel_call(
        body,
        (query, *blocks, out_slices, gain_row),
        tuple(shapes),
        flops=2 * tokens * columns * features * (group - 1),
        moved=2 * columns * features * (group - 1),
        limit=6,
    )


def project_own(attended, out_slices):
    tokens, columns = attended.shape
    features = out_slices.shape[1]

    def body(attended_ref, out_ref, own_ref):
        for start, width in tiles(features, 512):
            own_ref[:, start : start + width] = dot(
                attended_ref[...], out_ref[:, start : start + width]
            ).astype(BF16)

    return kernel_call(
        body,
        (attended, out_slices),
        struct((tokens, features), BF16),
        flops=2 * tokens * columns * features,
        moved=2 * columns * features,
        limit=4,
    )


def packing(features, experts):
    used = experts * CAPACITY
    rows = max(ROWS, 1 << (used - 1).bit_length())
    spare = rows - used
    if spare and used % spare == 0 and features % ((used // spare + 1) * 128) == 0:
        count = used // spare
        return rows, used, spare, count, features // (count + 1)
    return rows, used, 0, 1, features


def one_hot(hit):
    return hit.astype(F32).astype(BF16)


def placement(picked, layout, devices, experts):
    rows, used, spare, count, _ = layout
    tokens = picked.shape[1]
    expert = lax.broadcasted_iota(jnp.int32, (devices * experts, tokens), 0)
    chosen = expert == picked
    earlier = lax.broadcasted_iota(jnp.int32, (tokens, tokens), 0) < lax.broadcasted_iota(
        jnp.int32, (tokens, tokens), 1
    )
    before = dot(one_hot(chosen), one_hot(earlier))
    rank = jnp.sum(jnp.where(chosen, before, 0.0), axis=0, keepdims=True).astype(jnp.int32)
    target = lax.div(picked, jnp.full_like(picked, experts))
    slot = (picked - target * experts) * CAPACITY + rank
    row = lax.broadcasted_iota(jnp.int32, (devices * rows, tokens), 0)
    base = row - target * rows
    main = one_hot(base == slot)
    last = []
    for tile in range(count if spare else 0):
        within = slot - tile * spare
        last.append(one_hot((within >= 0) & (within < spare) & (base == used + within)))
    return main, last


def selection(expert, layout, devices, tile):
    rows, used, spare, _, _ = layout
    many, all_rows = devices * CAPACITY, devices * rows
    packed = lax.broadcasted_iota(jnp.int32, (many, all_rows), 0)
    arrived = lax.broadcasted_iota(jnp.int32, (many, all_rows), 1)
    source = arrived >> (rows.bit_length() - 1)
    slot = arrived & (rows - 1)
    if tile is None:
        fits = slot < used
    else:
        slot = slot - used
        fits = (slot >= 0) & (slot < spare)
        slot = slot + tile * spare
    within = slot - expert * CAPACITY
    hit = fits & (within >= 0) & (within < CAPACITY) & (packed == source * CAPACITY + within)
    return one_hot(hit)


def spreading(layout, experts, devices, tile):
    rows, used, spare, _, _ = layout
    many = devices * CAPACITY
    shape = (devices * rows, experts * many)
    row = lax.broadcasted_iota(jnp.int32, shape, 0)
    packed = lax.broadcasted_iota(jnp.int32, shape, 1)
    source = row >> (rows.bit_length() - 1)
    slot = row & (rows - 1)
    if tile is None:
        fits = slot < used
    else:
        slot = slot - used
        fits = (slot >= 0) & (slot < spare)
        slot = slot + tile * spare
    hit = None
    for expert in range(experts):
        within = slot - expert * CAPACITY
        here = (within >= 0) & (within < CAPACITY)
        here = here & (packed == expert * many + source * CAPACITY + within)
        hit = here if hit is None else hit | here
    return one_hot(fits & hit)


def tile_of(ref, layout, tile):
    rows = layout[0]
    value = ref[:, tile * rows : (tile + 1) * rows, :]
    return value.reshape(value.shape[0] * rows, value.shape[2])


def piece(layout, index):
    return slice(index * layout[4], (index + 1) * layout[4])


def dispatch(own, received, residual_in, gain_row, places, layout):
    devices = lax.axis_size("seq")
    tokens, features = own.shape
    count = len(received)
    rows, _, spare, tile_count, width = layout

    def body(*refs):
        own_ref, received_refs = refs[0], refs[1 : 1 + count]
        residual_ref, gain_ref, places_ref = refs[1 + count : 4 + count]
        total_ref, outgoing_ref = refs[4 + count :]

        def scaled(index):
            part = piece(layout, index)
            attention = own_ref[:, part].astype(F32)
            for received_ref in received_refs:
                attention = attention + received_ref[:tokens, part].astype(F32)
            residual = residual_ref[:, part].astype(F32) + attention
            total_ref[:, part] = residual
            return (residual * gain_ref[:, part]).astype(BF16)

        final = scaled(tile_count) if spare else None
        for tile in range(tile_count):
            laid = dot(places_ref[0], scaled(tile))
            if spare:
                laid = laid + dot(places_ref[1 + tile], final)
            outgoing_ref[:, tile * rows : (tile + 1) * rows, :] = laid.astype(BF16).reshape(
                devices, rows, width
            )

    return kernel_call(
        body,
        (own, *received, residual_in, gain_row, places),
        (
            struct((tokens, features), F32),
            struct((devices, tile_count * rows, width), BF16),
        ),
        limit=7,
    )


def take_rows(arrived_ref, take_ref, rows_ref, layout):
    _, _, spare, tile_count, _ = layout
    many = rows_ref.shape[0]
    final = None
    for tile in range(tile_count):
        taken = dot(take_ref[tile], tile_of(arrived_ref, layout, tile))
        rows_ref[:, piece(layout, tile)] = taken[:many].astype(BF16)
        if spare:
            final = taken[many:] if final is None else final + taken[many:]
    if spare:
        rows_ref[:, piece(layout, tile_count)] = final.astype(BF16)


def row_statistics(rows_ref, of_expert, gain, router_row):
    squares = logits = None
    inverse = 1.0 / gain
    for start, width in tiles(rows_ref.shape[1], 128):
        part = slice(start, start + width)
        row = rows_ref[of_expert, part].astype(F32)
        plain = row * inverse[:, part]
        product = row * router_row[:, part]
        squares = plain * plain if squares is None else squares + plain * plain
        logits = product if logits is None else logits + product
    return jnp.sum(squares, axis=1, keepdims=True), jnp.sum(logits, axis=1, keepdims=True)


def two_columns(first, second, rows):
    lane = lax.broadcasted_iota(jnp.int32, (rows, 128), 1)
    return jnp.where(lane == 0, first, jnp.where(lane == 1, second, 0.0))


def own_features(arrived, take, slices, gain_row, router_rows, layout):
    devices = lax.axis_size("seq")
    experts = len(slices) // 2
    features, hidden = slices[0].shape
    many = devices * CAPACITY

    def body(*refs):
        arrived_ref, take_ref, gain_ref, router_ref = refs[:4]
        up_refs, gate_refs = refs[4 : 4 + experts], refs[4 + experts : 4 + 2 * experts]
        gates, ups, stats, rows_ref = refs[4 + 2 * experts :]
        me = lax.axis_index("exp")
        columns = pl.ds(pl.multiple_of(me * features, 128), features)
        take_rows(arrived_ref, take_ref, rows_ref, layout)
        for expert in range(experts):
            of_expert = slice(expert * many, (expert + 1) * many)
            router_row = router_ref[expert : expert + 1, columns].astype(F32)
            stats[expert] = two_columns(
                *row_statistics(rows_ref, of_expert, gain_ref[...], router_row), many
            )
            for start, width in tiles(hidden, 256):
                part = slice(start, start + width)
                gates[expert, :, part] = dot(rows_ref[of_expert, :], gate_refs[expert][:, part])
                ups[expert, :, part] = dot(rows_ref[of_expert, :], up_refs[expert][:, part])

    return kernel_call(
        body,
        (arrived, take, gain_row, router_rows, *slices),
        (
            pltpu.VMEM((experts, many, hidden), F32),
            pltpu.VMEM((experts, many, hidden), F32),
            pltpu.VMEM((experts, many, 128), F32),
        ),
        scratch=[pltpu.VMEM((experts * many, features), BF16)],
        flops=4 * experts * many * features * hidden,
        moved=4 * experts * features * hidden,
        limit=8,
    )


def down_copies(down_ref, buffers, sems, first, target, features):
    columns = pl.ds(pl.multiple_of(target * features, 128), features)
    return [
        pltpu.make_async_copy(down_ref.at[expert, :, columns], buffer, sems.at[first + expert])
        for expert, buffer in enumerate(buffers)
    ]


def expand_rows(hidden_ref, down_refs, copies, spread_ref, laid_ref, target_ref, layout):
    rows, _, spare, tile_count, width = layout
    experts, many, _ = hidden_ref.shape
    devices = target_ref.shape[0]
    for expert in range(experts):
        copies[expert].wait()
        for index in range(laid_ref.shape[0]):
            laid_ref[index, expert * many : (expert + 1) * many, :] = dot(
                hidden_ref[expert], down_refs[expert][:, piece(layout, index)]
            ).astype(BF16)
    for tile in range(tile_count):
        laid = dot(spread_ref[tile, :, : experts * many], laid_ref[tile])
        if spare:
            laid = laid + dot(spread_ref[tile, :, experts * many :], laid_ref[tile_count])
        target_ref[:, tile * rows : (tile + 1) * rows, :] = laid.astype(BF16).reshape(
            devices, rows, width
        )


def laid_scratch(layout, experts, many):
    return pltpu.VMEM((layout[3] + (1 if layout[2] else 0), experts * many, layout[4]), BF16)


def other_features(
    arrivals,
    take,
    spread,
    gate_slices,
    up_weight,
    gains,
    router_rows,
    sums,
    down_weight,
    tokens,
    layout,
):
    devices, group = lax.axis_size("seq"), lax.axis_size("exp")
    experts = down_weight.shape[0]
    features, hidden = gate_slices[0].shape
    many = devices * CAPACITY
    count = group - 1
    width_all = features * group

    def body(*refs):
        arrived_refs, refs = refs[:count], refs[count:]
        gain_refs, refs = refs[:count], refs[count:]
        take_ref, spread_ref, router_ref, gates, ups, stats = refs[:6]
        gate_refs, refs = refs[6 : 6 + count * experts], refs[6 + count * experts :]
        up_from, down_ref, hidden_ref = refs[:3]
        send_refs = refs[3 : 3 + count]
        rows_ref, laid_ref, up_ref, buffer, up_sems, sems = refs[3 + count :]
        buffers = [buffer.at[index] for index in range(count * experts)]
        me = lax.axis_index("exp")
        up_copies = []
        for k in range(count):
            part = pl.ds(
                pl.multiple_of(lax.rem(me + group - k - 1, group) * features, 128), features
            )
            for expert in range(experts):
                index = k * experts + expert
                up_copies.append(
                    pltpu.make_async_copy(
                        up_from.at[expert, part, :], up_ref.at[index], up_sems.at[index]
                    )
                )
        for copy in up_copies:
            copy.start()
        copies = [
            down_copies(
                down_ref,
                buffers[k * experts : (k + 1) * experts],
                sems,
                k * experts,
                lax.rem(me + k + 1, group),
                features,
            )
            for k in range(count)
        ]
        for copy in [copy for some in copies for copy in some]:
            copy.start()
        statistics = [(stats[e][:, 0:1], stats[e][:, 1:2]) for e in range(experts)]
        for k in range(count):
            behind = lax.rem(me + group - k - 1, group)
            columns = pl.ds(pl.multiple_of(behind * features, 128), features)
            take_rows(arrived_refs[k], take_ref, rows_ref, layout)
            pair = gain_refs[k][tokens : tokens + ROWS, :].astype(F32)
            gain = pair[0:1, :] + pair[1:2, :]
            for expert in range(experts):
                of_expert = slice(expert * many, (expert + 1) * many)
                more = row_statistics(
                    rows_ref,
                    of_expert,
                    gain,
                    router_ref[expert : expert + 1, columns].astype(F32),
                )
                statistics[expert] = [a + b for a, b in zip(statistics[expert], more)]
                squares, logits = statistics[expert]
                scale = lax.rsqrt(squares / width_all + EPSILON)
                router_gate = 1.0 / (1.0 + jnp.exp(-(logits * scale)))
                for start, size in tiles(hidden, 256):
                    part = slice(start, start + size)
                    gate = gates[expert, :, part] + dot(
                        rows_ref[of_expert, :], gate_refs[k * experts + expert][:, part]
                    )
                    if k == count - 1:
                        gate = gate * scale
                        gate = gate / (1.0 + jnp.exp(-gate)) * (scale * router_gate)
                    gates[expert, :, part] = gate
            for expert in range(experts):
                of_expert = slice(expert * many, (expert + 1) * many)
                index = k * experts + expert
                up_copies[index].wait()
                for start, size in tiles(hidden, 256):
                    part = slice(start, start + size)
                    up = ups[expert, :, part] + dot(
                        rows_ref[of_expert, :], up_ref[index, :, part]
                    )
                    if k < count - 1:
                        ups[expert, :, part] = up
                    else:
                        hidden_ref[expert, :, part] = (gates[expert, :, part] * up).astype(BF16)
        for k in range(count):
            down_refs = buffers[k * experts : (k + 1) * experts]
            expand_rows(
                hidden_ref, down_refs, copies[k], spread_ref, laid_ref, send_refs[k], layout
            )

    rows, _, _, tile_count, width = layout
    ins = (*arrivals, *gains, take, spread, router_rows, *sums, *gate_slices)
    return kernel_call(
        body,
        (*ins, up_weight, down_weight),
        (
            pltpu.VMEM((experts, many, hidden), BF16),
            *[pltpu.VMEM((devices, tile_count * rows, width), BF16)] * count,
        ),
        specs=[VMEM] * len(ins) + [ANY] * 2,
        scratch=[
            pltpu.VMEM((experts * many, features), BF16),
            laid_scratch(layout, experts, many),
            pltpu.VMEM((count * experts, features, hidden), BF16),
            pltpu.VMEM((count * experts, hidden, features), BF16),
            pltpu.SemaphoreType.DMA((count * experts,)),
            pltpu.SemaphoreType.DMA((count * experts,)),
        ],
        flops=6 * experts * many * features * hidden,
        moved=6 * experts * features * hidden,
        limit=30,
    )


def own_outputs(hidden_rows, down_weight, spread, features, layout):
    devices = lax.axis_size("seq")
    rows, _, _, tile_count, width = layout
    experts, many, hidden = hidden_rows.shape

    def body(hidden_ref, spread_ref, down_ref, own_ref, laid_ref, buffer, sems):
        buffers = [buffer.at[expert] for expert in range(experts)]
        copies = down_copies(down_ref, buffers, sems, 0, lax.axis_index("exp"), features)
        for copy in copies:
            copy.start()
        expand_rows(hidden_ref, buffers, copies, spread_ref, laid_ref, own_ref, layout)

    return kernel_call(
        body,
        (hidden_rows, spread, down_weight),
        struct((devices, tile_count * rows, width), BF16),
        specs=[VMEM] * 2 + [ANY],
        scratch=[
            laid_scratch(layout, experts, many),
            pltpu.VMEM((experts, hidden, features), BF16),
            pltpu.SemaphoreType.DMA((experts,)),
        ],
        flops=2 * experts * many * features * hidden,
        moved=2 * experts * features * hidden,
        limit=20,
    )


def add_groups(own, received):
    def body(*refs):
        total = refs[0][...].astype(F32)
        for ref in refs[1:-1]:
            total = total + ref[...].astype(F32)
        refs[-1][...] = total.astype(BF16)

    return kernel_call(body, (own, *received), struct(own.shape, BF16), limit=8)


def finish(residual, returned, places, layout):
    tokens, features = residual.shape
    _, _, spare, tile_count, _ = layout

    def body(residual_ref, returned_ref, places_ref, out_ref):
        final = None
        for tile in range(tile_count):
            value = tile_of(returned_ref, layout, tile)
            part = piece(layout, tile)
            routed = dot(places_ref[0], value, ((0,), (0,)))
            out_ref[:, part] = (residual_ref[:, part] + routed).astype(BF16)
            if spare:
                more = dot(places_ref[1 + tile], value, ((0,), (0,)))
                final = more if final is None else final + more
        if spare:
            part = piece(layout, tile_count)
            out_ref[:, part] = (residual_ref[:, part] + final).astype(BF16)

    return kernel_call(
        body,
        (residual, returned, places),
        struct((tokens, features), BF16),
        limit=8,
    )


def local(
    query_input,
    key_input,
    value_input,
    segment_ids,
    residual_in,
    out_weight,
    norm_gain,
    router,
    modality,
    expert_in,
    gate_weight,
    up_weight,
    down_weight,
):
    tokens, columns = query_input.shape
    features = residual_in.shape[1]
    devices, group = lax.axis_size("seq"), lax.axis_size("exp")
    experts = gate_weight.shape[0]
    layout = packing(features, experts)
    gain_row = norm_gain.reshape(1, features)
    router_rows = router.T
    modality, expert_in = modality.reshape(1, tokens), expert_in.reshape(1, tokens)

    def held(value):
        return pltpu.with_memory_space_constraint(value, pltpu.VMEM)

    out_weight = pltpu.with_memory_space_constraint(out_weight, pltpu.HBM)
    gate_weight = pltpu.with_memory_space_constraint(gate_weight, pltpu.HBM)
    up_weight = pltpu.with_memory_space_constraint(up_weight, pltpu.HBM)
    down_weight = pltpu.with_memory_space_constraint(down_weight, pltpu.HBM)
    packed = pack_keys(key_input, value_input, segment_ids.reshape(1, tokens))
    blocks = [shifted(packed, "seq", step) for step in range(1, devices // 8 + 1)]
    prepared = prepare(
        out_weight, gate_weight, up_weight, modality, expert_in, features, layout
    )
    out_own, out_others, places, take, spread, *slices = [held(value) for value in prepared]
    attended, *contributions = attend(query_input, [packed, *blocks], out_others, gain_row)
    received = [rotated(value, "exp", k + 1) for k, value in enumerate(contributions)]
    own = project_own(attended, out_own)
    residual, outgoing = dispatch(own, received, residual_in, gain_row, places, layout)

    def exchanged(value):
        return lax.all_to_all(value, "seq", split_axis=0, concat_axis=0, tiled=True)

    arrived = exchanged(outgoing)
    arrivals = [rotated(arrived, "exp", k) for k in range(1, group)]
    sums = own_features(
        arrived, take, slices[: 2 * experts], gain_row, router_rows, layout
    )
    hidden_rows, *partials = other_features(
        arrivals,
        take,
        spread,
        slices[2 * experts :],
        up_weight,
        received,
        router_rows,
        [held(value) for value in sums],
        down_weight,
        tokens,
        layout,
    )
    hidden_rows = held(hidden_rows)
    others = [rotated(value, "exp", k + 1) for k, value in enumerate(partials)]
    own_part = own_outputs(hidden_rows, down_weight, spread, features, layout)
    returned = exchanged(add_groups(own_part, others))
    return finish(residual, returned, places, layout)


def solution(mesh):
    in_specs = (
        P("seq", "exp"),
        P("seq", "exp"),
        P("seq", "exp"),
        P("seq"),
        P("seq", "exp"),
        P("exp", None),
        P("exp"),
        P(None, "seq"),
        P("seq"),
        P("seq"),
        P("seq", None, "exp"),
        P("seq", None, "exp"),
        P("seq", "exp", None),
    )
    return jax.shard_map(
        local, mesh=mesh, in_specs=in_specs, out_specs=P("seq", "exp"), check_vma=False
    )
```

time: 157 us -> 124 us (0.79)
  local copies, waits for them, and re-layouts: 35.3 us -> 3.96 us
  waiting for transfers between devices: 1.25 us -> 5.64 us
  blocking collectives: 62.5 us -> 59.1 us
  other arithmetic: 1.72 us -> 0 us
    unnamed x34 -> x16, local copies, waits for them, and re-layouts: 35.2 us -> 3.96 us
    ppermute x2, waiting for transfers between devices: 0.01 us -> 4.38 us  [shifted(): lax.ppermute(value, axis, [(source, source + steps) for source in range(l...]
    all_to_all x2, blocking collectives: 62.5 us -> 59.1 us  [exchanged(): return lax.all_to_all(value, 'seq', split_axis=0, concat_axis=0, tiled=True)]
    pallas_call x9 -> x10, Pallas kernels: 47 us -> 45.9 us  [kernel_call(): pl.pallas_call(body, in_specs=specs, out_specs=outs, out_shape=out_shape,...]
  transfers between devices with their start and end apart: 5 -> 5, of which waited for: 1 -> 2; matrix products, arithmetic and copies ran while one was open for 0% -> 0% of each run, Pallas kernels for 18% -> 21%
where the time goes in v2:
time: 124 us
  blocking collectives  59.1 us (48%)
  Pallas kernels  45.9 us (37%)
  starting transfers between devices  8.99 us (7%)
  waiting for transfers between devices  5.64 us (5%)
  local copies, waits for them, and re-layouts  3.96 us (3%)
    all_to_all x2, blocking collectives, exchanged(): return lax.all_to_all(value, 'seq', split_axis=0, concat_axis=0, tiled=True)  59.1 us
    pallas_call x10, Pallas kernels, kernel_call(): pl.pallas_call(body, in_specs=specs, out_specs=outs, out_shape=out_shape,...  45.9 us
    ppermute x2, starting transfers between devices, shifted(): lax.ppermute(value, axis, [(source, source + steps) for source in range(l...  8.34 us
    ppermute x2, waiting for transfers between devices, shifted(): lax.ppermute(value, axis, [(source, source + steps) for source in range(l...  4.38 us
    unnamed x16, local copies, waits for them, and re-layouts  3.96 us
  transfers between devices with their start and end apart: 5, of which 2 were waited for; matrix products, arithmetic and copies ran while one was open for 0% of the time, Pallas kernels for 21%

profile of v2, /device:TPU:0, one launch (start us, length us, event | category | flops | bytes accessed | tf_op | source)
XLA Modules:
  0.0 123.8 jit_solution(17473642557656619411)
XLA Ops:
  0.0 1.1 shard_map.127.refs_1_
  1.1 4.9 %collective-permute-start.1 = (bf16[272,1024]{1,0:T(8,128)(2,1)S(1)}, bf16[272,1024]{1,0:T(8,128)(2,1)S(1)}, u32[]{:S(2)}, u32[]{:S(2)}) collective-permute-start(bf16[272,1024]{1,0:T(8,128)(2,1)S(1)} %shard_map.127.refs_1_), channel_id=1, source_target_pairs={{0,4},{2,6},{4,8},{6,10},{8,12},{10,14},{12,16},{14,18},{16,20},{1... | collective-permute-start | bytes 1671176 | tf_op jit(solution)/shard_map/ppermute | solution.py:36
  6.0 3.4 %collective-permute-start = (bf16[272,1024]{1,0:T(8,128)(2,1)S(1)}, bf16[272,1024]{1,0:T(8,128)(2,1)S(1)}, u32[]{:S(2)}, u32[]{:S(2)}) collective-permute-start(bf16[272,1024]{1,0:T(8,128)(2,1)S(1)} %shard_map.127.refs_1_), channel_id=1, source_target_pairs={{0,2},{2,4},{4,6},{6,8},{8,10},{10,12},{12,14},{14,16},{16,18},{18... | collective-permute-start | bytes 1671176 | tf_op jit(solution)/shard_map/ppermute | solution.py:36
  9.4 0.0 copy-start.6
  9.4 0.6 copy-done.6
  10.1 0.7 copy-done.7
  10.7 14.6 %shard_map.128 = (bf16[1024,2048]{1,0:T(8,128)(2,1)S(1)}, bf16[1,1024,2048]{2,1,0:T(8,128)(2,1)S(1)}, bf16[8,256,128]{2,1,0:T(8,128)(2,1)S(1)}, bf16[7,448,256]{...) custom-call(bf16[1024,4096]{1,0:T(8,128)(2,1)} %refs_0_.2, ...), custom_call_target="tpu_custom_call" | custom-call | bytes 54525952 | tf_op jit(solution)/shard_map/pallas_call | solution.py:51
  25.4 0.0 copy-start
  25.4 0.0 copy-start.2
  25.4 4.4 %collective-permute-done.1.refs_3_ = bf16[272,1024]{1,0:T(8,128)(2,1)S(1)} collective-permute-done((bf16[272,1024]{1,0:T(8,128)(2,1)S(1)}, bf16[272,1024]{1,0:T(8,128)(2,1)S(1)}, u32[]{:S(2)}, u32[]{:S(2)}) %collective-permute-start.1) | collective-permute-done | bytes 557088 | tf_op jit(solution)/shard_map/ppermute | solution.py:36
  29.8 0.0 collective-permute-done.refs_2_
  29.8 0.0 copy-done.4
  29.8 3.1 %shard_map.129 = (bf16[128,1024]{1,0:T(8,128)(2,1)S(1)}, bf16[144,2048]{1,0:T(8,128)(2,1)S(1)}) custom-call(bf16[128,1024]{1,0:T(8,128)(2,1)S(1)} %copy-done.3, bf16[272,1024]{1,0:T(8,128)(2,1)S(1)} %shard_map.127.refs_1_, bf16[272,1024]{1,0:T(8,128)(2,1)S(1)} %collective-permute-done.refs_2_, bf16[272,1024]{1,0:T(8,128)(2,1)S(1)} %collective-permute-done.1.refs_3_, ...), custom_call_target="tpu_custom_call" | custom-call | flops 536870912 | bytes 4194304 | tf_op jit(solution)/shard_map/pallas_call | solution.py:51
  32.9 0.0 copy-start.5
  32.9 0.1 collective-permute-start.2
  33.0 0.7 shard_map.130.refs_0_
  33.7 1.2 %collective-permute-done.2.refs_1_ = bf16[144,2048]{1,0:T(8,128)(2,1)S(1)} collective-permute-done((bf16[144,2048]{1,0:T(8,128)(2,1)S(1)}, bf16[144,2048]{1,0:T(8,128)(2,1)S(1)}, u32[]{:S(2)}, u32[]{:S(2)}) %collective-permute-start.2) | collective-permute-done | bytes 589856 | tf_op jit(solution)/shard_map/ppermute | solution.py:41
  35.0 0.0 copy-done.2
  35.0 0.7 shard_map.131
  35.6 0.0 copy-done
  35.7 31.7 %all_to_all.10.refs_0_ = bf16[16,112,256]{2,1,0:T(8,128)(2,1)S(1)} all-to-all(bf16[16,112,256]{2,1,0:T(8,128)(2,1)S(1)} %get-tuple-element.31), channel_id=1, replica_groups=mesh['seq'=16,'exp'=2] {'seq'}, dimensions={0} | all-to-all | bytes 1835008 | tf_op jit(solution)/shard_map/all_to_all | solution.py:720
  67.3 0.0 collective-permute-start.3
  67.4 4.8 %shard_map.132 = (f32[2,112,1408]{2,1,0:T(8,128)S(1)}, f32[2,112,1408]{2,1,0:T(8,128)S(1)}, f32[2,112,128]{2,1,0:T(8,128)S(1)}) custom-call(bf16[16,112,256]{2,1,0:T(8,128)(2,1)S(1)} %all_to_all.10.refs_0_, bf16[7,448,256]{2,1,0:T(8,128)(2,1)S(1)} %get-tuple-element.32.refs_1_.refs_2_, f32[1,2048]{1,0:T(1,128)S(1)} %bitcast.7, bf16[2,4096]{1,0:T(2,128)(2,1)S(1)} %bitcast.8, ...), custom_call_target="tpu_custom_call" | custom-call | flops 2583691264 | bytes 23068672 | tf_op jit(solution)/shard_map/pallas_call | solution.py:51
  72.1 0.0 collective-permute-done.3.refs_0_
  72.1 2.6 %copy-done.1 = bf16[2048,1408]{1,0:T(8,128)(2,1)S(1)} copy-done((bf16[2048,1408]{1,0:T(8,128)(2,1)S(1)}, bf16[2048,1408]{1,0:T(8,128)(2,1)}, u32[]{:S(2)}) %copy-start.1) | copy-done | bytes 5767192
  74.8 13.5 %shard_map.133 = (bf16[2,112,1408]{2,1,0:T(8,128)(2,1)S(1)}, bf16[16,112,256]{2,1,0:T(8,128)(2,1)S(1)}) custom-call(bf16[16,112,256]{2,1,0:T(8,128)(2,1)S(1)} %collective-permute-done.3.refs_0_, bf16[144,2048]{1,0:T(8,128)(2,1)S(1)} %collective-permute-done.2.refs_1_, bf16[7,448,256]{2,1,0:T(8,128)(2,1)S(1)} %get-tuple-element.32.refs_1_.refs_2_, ...), custom_call_target="tpu_custom_call" | custom-call | flops 3875536896 | bytes 34603008 | tf_op jit(solution)/shard_map/pallas_call | solution.py:51
  88.3 0.6 collective-permute-start.4
  88.9 6.0 %shard_map.134.refs_0_ = bf16[16,112,256]{2,1,0:T(8,128)(2,1)S(1)} custom-call(bf16[2,112,1408]{2,1,0:T(8,128)(2,1)S(1)} %get-tuple-element.43.hidden_ref, bf16[7,256,448]{2,1,0:T(8,128)(2,1)S(1)} %get-tuple-element.33.refs_3_.spread_ref, bf16[2,1408,4096]{2,1,0:T(8,128)(2,1)} %down_ref.1), custom_call_target="tpu_custom_call" | custom-call | flops 1291845632 | bytes 11534336 | tf_op jit(solution)/shard_map/pallas_call | solution.py:51
  94.8 0.0 collective-permute-done.4.refs_1_
  94.8 0.2 shard_map.135
  95.1 27.4 %all_to_all.11.returned_ref = bf16[16,112,256]{2,1,0:T(8,128)(2,1)S(1)} all-to-all(bf16[16,112,256]{2,1,0:T(8,128)(2,1)S(1)} %shard_map.135), channel_id=1, replica_groups=mesh['seq'=16,'exp'=2] {'seq'}, dimensions={0} | all-to-all | bytes 1835008 | tf_op jit(solution)/shard_map/all_to_all | solution.py:720
  122.5 1.3 %shard_map.136 = bf16[128,2048]{1,0:T(8,128)(2,1)} custom-call(f32[128,2048]{1,0:T(8,128)S(1)} %get-tuple-element.30.residual_ref, bf16[16,112,256]{2,1,0:T(8,128)(2,1)S(1)} %all_to_all.11.returned_ref, bf16[8,256,128]{2,1,0:T(8,128)(2,1)S(1)} %get-tuple-element.29.refs_4_.places_ref), custom_call_target="tpu_custom_call" | custom-call | tf_op jit(solution)/shard_map/pallas_call | solution.py:51
  (6 shorter events, 0.0 us)
Async XLA Ops:
  1.1 28.7 %collective-permute-start.1 = (bf16[272,1024]{1,0:T(8,128)(2,1)S(1)}, bf16[272,1024]{1,0:T(8,128)(2,1)S(1)}, u32[]{:S(2)}, u32[]{:S(2)}) collective-permute-start(bf16[272,1024]{1,0:T(8,128)(2,1)S(1)} %shard_map.127.refs_1_), channel_id=1, source_target_pairs={{0,4},{2,6},{4,8},{6,10},{8,12},{10,14},{12,16},{14,18},{16,20},{1... | collective-permute-start | bytes 1671176 | tf_op jit(solution)/shard_map/ppermute | solution.py:36
  6.0 23.8 %collective-permute-start = (bf16[272,1024]{1,0:T(8,128)(2,1)S(1)}, bf16[272,1024]{1,0:T(8,128)(2,1)S(1)}, u32[]{:S(2)}, u32[]{:S(2)}) collective-permute-start(bf16[272,1024]{1,0:T(8,128)(2,1)S(1)} %shard_map.127.refs_1_), channel_id=1, source_target_pairs={{0,2},{2,4},{4,6},{6,8},{8,10},{10,12},{12,14},{14,16},{16,18},{18... | collective-permute-start | bytes 1671176 | tf_op jit(solution)/shard_map/ppermute | solution.py:36
  9.4 0.7 copy-start.6
  10.1 0.7 copy-start.7
  10.7 19.0 %copy-start.3 = (bf16[128,1024]{1,0:T(8,128)(2,1)S(1)}, bf16[128,1024]{1,0:T(8,128)(2,1)}, u32[]{:S(2)}) copy-start(bf16[128,1024]{1,0:T(8,128)(2,1)} %refs_0_.3) | copy-start | bytes 786436
  10.7 19.0 %copy-start.4 = (f32[2048]{0:T(1024)S(1)}, f32[2048]{0:T(1024)}, u32[]{:S(2)}) copy-start(f32[2048]{0:T(1024)} %param.19) | copy-start | bytes 24580
  25.4 10.3 %copy-start = (bf16[2048,1408]{1,0:T(8,128)(2,1)}, bf16[2048,1408]{1,0:T(8,128)(2,1)S(1)}, u32[]{:S(2)}) copy-start(bf16[2048,1408]{1,0:T(8,128)(2,1)S(1)} %get-tuple-element.41.refs_8_) | copy-start | bytes 17301508
  25.4 9.6 %copy-start.2 = (bf16[128,2048]{1,0:T(8,128)(2,1)S(1)}, bf16[128,2048]{1,0:T(8,128)(2,1)}, u32[]{:S(2)}) copy-start(bf16[128,2048]{1,0:T(8,128)(2,1)} %refs_2_.3) | copy-start | bytes 1572868
  32.9 34.5 %copy-start.5 = (bf16[4096,2]{0,1:T(2,128)(2,1)S(1)}, bf16[4096,2]{0,1:T(2,128)(2,1)}, u32[]{:S(2)}) copy-start(bf16[4096,2]{0,1:T(2,128)(2,1)} %param.20) | copy-start | bytes 49156
  32.9 2.1 %collective-permute-start.2 = (bf16[144,2048]{1,0:T(8,128)(2,1)S(1)}, bf16[144,2048]{1,0:T(8,128)(2,1)S(1)}, u32[]{:S(2)}, u32[]{:S(2)}) collective-permute-start(bf16[144,2048]{1,0:T(8,128)(2,1)S(1)} %get-tuple-element.28), channel_id=1, source_target_pairs={{0,1},{1,0},{2,3},{3,2},{4,5},{5,4},{6,7},{7,6},{8,9},{9,8},{10,11... | collective-permute-start | bytes 1769480 | tf_op jit(solution)/shard_map/ppermute | solution.py:41
  67.3 4.8 %collective-permute-start.3 = (bf16[16,112,256]{2,1,0:T(8,128)(2,1)S(1)}, bf16[16,112,256]{2,1,0:T(8,128)(2,1)S(1)}, u32[]{:S(2)}, u32[]{:S(2)}) collective-permute-start(bf16[16,112,256]{2,1,0:T(8,128)(2,1)S(1)} %all_to_all.10.refs_0_), channel_id=1, source_target_pairs={{0,1},{1,0},{2,3},{3,2},{4,5},{5,4},{6,7},{7,6},{8,9},{9,8},{10,11... | collective-permute-start | bytes 2752520 | tf_op jit(solution)/shard_map/ppermute | solution.py:41
  72.1 2.6 %copy-start.1 = (bf16[2048,1408]{1,0:T(8,128)(2,1)S(1)}, bf16[2048,1408]{1,0:T(8,128)(2,1)}, u32[]{:S(2)}) copy-start(bf16[2048,1408]{1,0:T(8,128)(2,1)} %copy-done) | copy-start | bytes 17301508
  88.3 6.6 %collective-permute-start.4 = (bf16[16,112,256]{2,1,0:T(8,128)(2,1)S(1)}, bf16[16,112,256]{2,1,0:T(8,128)(2,1)S(1)}, u32[]{:S(2)}, u32[]{:S(2)}) collective-permute-start(bf16[16,112,256]{2,1,0:T(8,128)(2,1)S(1)} %get-tuple-element.44), channel_id=1, source_target_pairs={{0,1},{1,0},{2,3},{3,2},{4,5},{5,4},{6,7},{7,6},{8,9},{9,8},{10,11... | collective-permute-start | bytes 2752520 | tf_op jit(solution)/shard_map/ppermute | solution.py:41

commit v3 on v2

--- a/solution.py
+++ b/solution.py
@@ -117,10 +117,8 @@
             ahead = lax.rem(me + k, group)
             columns = pl.ds(pl.multiple_of(ahead * feature_count, 128), feature_count)
             copies.append((out_ref.at[:, columns], out_others.at[k - 1] if k else out_own))
-        wanted = [(up_ref, 0)] + [(gate_ref, k) for k in range(group)]
-        for which, (ref, k) in enumerate(wanted):
-            behind = lax.rem(me + group - k, group)
-            part = pl.ds(pl.multiple_of(behind * feature_count, 128), feature_count)
+        part = pl.ds(pl.multiple_of(me * feature_count, 128), feature_count)
+        for which, ref in enumerate((up_ref, gate_ref)):
             for expert in range(experts):
                 copies.append((ref.at[expert, part, :], slices[which * experts + expert]))
         started = [
@@ -154,14 +152,14 @@
         pltpu.VMEM((1 + (tile_count if spare else 0), devices * rows, tokens), BF16),
         pltpu.VMEM((tile_count, kinds * experts * many, devices * rows), BF16),
         pltpu.VMEM((tile_count, devices * rows, kinds * experts * many), BF16),
-        *[pltpu.VMEM((feature_count, hidden), BF16)] * ((1 + group) * experts),
+        *[pltpu.VMEM((feature_count, hidden), BF16)] * (2 * experts),
     )
     return kernel_call(
         body,
         (out_weight, gate_weight, up_weight, modality, expert_in),
         shapes,
         specs=[ANY] * 3 + [VMEM] * 2,
-        scratch=[pltpu.SemaphoreType.DMA((group + (1 + group) * experts,))],
+        scratch=[pltpu.SemaphoreType.DMA((group + 2 * experts,))],
         moved=2 * (out_weight.size + gate_weight.size + up_weight.size),
         limit=4,
     )
@@ -486,7 +484,7 @@
     arrivals,
     take,
     spread,
-    gate_slices,
+    gate_weight,
     up_weight,
     gains,
     router_rows,
@@ -497,7 +495,7 @@
 ):
     devices, group = lax.axis_size("seq"), lax.axis_size("exp")
     experts = down_weight.shape[0]
-    features, hidden = gate_slices[0].shape
+    features, hidden = gate_weight.shape[1] // group, gate_weight.shape[2]
     many = devices * CAPACITY
     count = group - 1
     width_all = features * group
@@ -506,25 +504,29 @@
         arrived_refs, refs = refs[:count], refs[count:]
         gain_refs, refs = refs[:count], refs[count:]
         take_ref, spread_ref, router_ref, gates, ups, stats = refs[:6]
-        gate_refs, refs = refs[6 : 6 + count * experts], refs[6 + count * experts :]
-        up_from, down_ref, hidden_ref = refs[:3]
-        send_refs = refs[3 : 3 + count]
-        rows_ref, laid_ref, up_ref, buffer, up_sems, sems = refs[3 + count :]
+        gate_from, up_from, down_ref, hidden_ref = refs[6:10]
+        send_refs = refs[10 : 10 + count]
+        rows_ref, laid_ref, gate_ref, up_ref, buffer, gate_sems, up_sems, sems = refs[10 + count :]
         buffers = [buffer.at[index] for index in range(count * experts)]
         me = lax.axis_index("exp")
-        up_copies = []
+        gate_copies, up_copies = [], []
         for k in range(count):
             part = pl.ds(
                 pl.multiple_of(lax.rem(me + group - k - 1, group) * features, 128), features
             )
             for expert in range(experts):
                 index = k * experts + expert
+                gate_copies.append(
+                    pltpu.make_async_copy(
+                        gate_from.at[expert, part, :], gate_ref.at[index], gate_sems.at[index]
+                    )
+                )
                 up_copies.append(
                     pltpu.make_async_copy(
                         up_from.at[expert, part, :], up_ref.at[index], up_sems.at[index]
                     )
                 )
-        for copy in up_copies:
+        for copy in gate_copies + up_copies:
             copy.start()
         copies = [
             down_copies(
@@ -558,10 +560,12 @@
                 squares, logits = statistics[expert]
                 scale = lax.rsqrt(squares / width_all + EPSILON)
                 router_gate = 1.0 / (1.0 + jnp.exp(-(logits * scale)))
+                index = k * experts + expert
+                gate_copies[index].wait()
                 for start, size in tiles(hidden, 256):
                     part = slice(start, start + size)
                     gate = gates[expert, :, part] + dot(
-                        rows_ref[of_expert, :], gate_refs[k * experts + expert][:, part]
+                        rows_ref[of_expert, :], gate_ref[index, :, part]
                     )
                     if k == count - 1:
                         gate = gate * scale
@@ -587,26 +591,28 @@
             )
 
     rows, _, _, tile_count, width = layout
-    ins = (*arrivals, *gains, take, spread, router_rows, *sums, *gate_slices)
-    return kernel_call(
-        body,
-        (*ins, up_weight, down_weight),
+    ins = (*arrivals, *gains, take, spread, router_rows, *sums)
+    return kernel_call(
+        body,
+        (*ins, gate_weight, up_weight, down_weight),
         (
             pltpu.VMEM((experts, many, hidden), BF16),
             *[pltpu.VMEM((devices, tile_count * rows, width), BF16)] * count,
         ),
-        specs=[VMEM] * len(ins) + [ANY] * 2,
+        specs=[VMEM] * len(ins) + [ANY] * 3,
         scratch=[
             pltpu.VMEM((experts * many, features), BF16),
             laid_scratch(layout, experts, many),
             pltpu.VMEM((count * experts, features, hidden), BF16),
+            pltpu.VMEM((count * experts, features, hidden), BF16),
             pltpu.VMEM((count * experts, hidden, features), BF16),
+            pltpu.SemaphoreType.DMA((count * experts,)),
             pltpu.SemaphoreType.DMA((count * experts,)),
             pltpu.SemaphoreType.DMA((count * experts,)),
         ],
         flops=6 * experts * many * features * hidden,
         moved=6 * experts * features * hidden,
-        limit=30,
+        limit=42,
     )
 
 
@@ -722,13 +728,13 @@
     arrived = exchanged(outgoing)
     arrivals = [rotated(arrived, "exp", k) for k in range(1, group)]
     sums = own_features(
-        arrived, take, slices[: 2 * experts], gain_row, router_rows, layout
+        arrived, take, slices, gain_row, router_rows, layout
     )
     hidden_rows, *partials = other_features(
         arrivals,
         take,
         spread,
-        slices[2 * experts :],
+        gate_weight,
         up_weight,
         received,
         router_rows,

time: 124 us -> 122 us (0.984)
  waiting for transfers between devices: 5.64 us -> 9.18 us
  local copies, waits for them, and re-layouts: 3.96 us -> 1.33 us
  Pallas kernels: 45.9 us -> 43.3 us
    ppermute x2, waiting for transfers between devices: 4.38 us -> 7.93 us  [shifted(): lax.ppermute(value, axis, [(source, source + steps) for source in range(l...]
    unnamed x16 -> x12, local copies, waits for them, and re-layouts: 3.96 us -> 1.33 us
    pallas_call x10, Pallas kernels: 45.9 us -> 43.3 us  [kernel_call(): pl.pallas_call(body, in_specs=specs, out_specs=outs, out_shape=out_shape,...]
  transfers between devices with their start and end apart: 5 -> 5, of which waited for: 2 -> 2; matrix products, arithmetic and copies ran while one was open for 0% -> 0% of each run, Pallas kernels for 21% -> 18%
where the time goes in v3:
time: 122 us
  blocking collectives  59.1 us (48%)
  Pallas kernels  43.3 us (35%)
  waiting for transfers between devices  9.18 us (8%)
  starting transfers between devices  8.98 us (7%)
  local copies, waits for them, and re-layouts  1.33 us (1%)
    all_to_all x2, blocking collectives, exchanged(): return lax.all_to_all(value, 'seq', split_axis=0, concat_axis=0, tiled=True)  59.1 us
    pallas_call x10, Pallas kernels, kernel_call(): pl.pallas_call(body, in_specs=specs, out_specs=outs, out_shape=out_shape,...  43.3 us
    ppermute x2, starting transfers between devices, shifted(): lax.ppermute(value, axis, [(source, source + steps) for source in range(l...  8.34 us
    ppermute x2, waiting for transfers between devices, shifted(): lax.ppermute(value, axis, [(source, source + steps) for source in range(l...  7.93 us
  transfers between devices with their start and end apart: 5, of which 2 were waited for; matrix products, arithmetic and copies ran while one was open for 0% of the time, Pallas kernels for 18%

profile of v3, /device:TPU:0, one launch (start us, length us, event | category | flops | bytes accessed | tf_op | source)
XLA Modules:
  0.0 122.1 jit_solution(14118492840434602267)
XLA Ops:
  0.0 1.1 shard_map.127.refs_1_
  1.1 4.9 %collective-permute-start.1 = (bf16[272,1024]{1,0:T(8,128)(2,1)S(1)}, bf16[272,1024]{1,0:T(8,128)(2,1)S(1)}, u32[]{:S(2)}, u32[]{:S(2)}) collective-permute-start(bf16[272,1024]{1,0:T(8,128)(2,1)S(1)} %shard_map.127.refs_1_), channel_id=1, source_target_pairs={{0,4},{2,6},{4,8},{6,10},{8,12},{10,14},{12,16},{14,18},{16,20},{1... | collective-permute-start | bytes 1671176 | tf_op jit(solution)/shard_map/ppermute | solution.py:36
  6.0 3.4 %collective-permute-start = (bf16[272,1024]{1,0:T(8,128)(2,1)S(1)}, bf16[272,1024]{1,0:T(8,128)(2,1)S(1)}, u32[]{:S(2)}, u32[]{:S(2)}) collective-permute-start(bf16[272,1024]{1,0:T(8,128)(2,1)S(1)} %shard_map.127.refs_1_), channel_id=1, source_target_pairs={{0,2},{2,4},{4,6},{6,8},{8,10},{10,12},{12,14},{14,16},{16,18},{18... | collective-permute-start | bytes 1671176 | tf_op jit(solution)/shard_map/ppermute | solution.py:36
  9.4 0.0 copy-start.4
  9.4 0.6 copy-done.4
  10.1 0.0 copy-start.5
  10.1 0.7 copy-done.5
  10.7 11.1 %shard_map.128 = (bf16[1024,2048]{1,0:T(8,128)(2,1)S(1)}, bf16[1,1024,2048]{2,1,0:T(8,128)(2,1)S(1)}, bf16[8,256,128]{2,1,0:T(8,128)(2,1)S(1)}, bf16[7,448,256]{...) custom-call(bf16[1024,4096]{1,0:T(8,128)(2,1)} %refs_0_.2, ...), custom_call_target="tpu_custom_call" | custom-call | bytes 54525952 | tf_op jit(solution)/shard_map/pallas_call | solution.py:51
  21.8 0.0 copy-start
  21.8 7.9 %collective-permute-done.1.refs_3_ = bf16[272,1024]{1,0:T(8,128)(2,1)S(1)} collective-permute-done((bf16[272,1024]{1,0:T(8,128)(2,1)S(1)}, bf16[272,1024]{1,0:T(8,128)(2,1)S(1)}, u32[]{:S(2)}, u32[]{:S(2)}) %collective-permute-start.1) | collective-permute-done | bytes 557088 | tf_op jit(solution)/shard_map/ppermute | solution.py:36
  29.8 0.0 collective-permute-done.refs_2_
  29.8 0.0 copy-done.1
  29.8 0.0 copy-done.2
  29.8 3.1 %shard_map.129 = (bf16[128,1024]{1,0:T(8,128)(2,1)S(1)}, bf16[144,2048]{1,0:T(8,128)(2,1)S(1)}) custom-call(bf16[128,1024]{1,0:T(8,128)(2,1)S(1)} %copy-done.1, bf16[272,1024]{1,0:T(8,128)(2,1)S(1)} %shard_map.127.refs_1_, bf16[272,1024]{1,0:T(8,128)(2,1)S(1)} %collective-permute-done.refs_2_, bf16[272,1024]{1,0:T(8,128)(2,1)S(1)} %collective-permute-done.1.refs_3_, ...), custom_call_target="tpu_custom_call" | custom-call | flops 536870912 | bytes 4194304 | tf_op jit(solution)/shard_map/pallas_call | solution.py:51
  32.9 0.0 copy-start.3
  32.9 0.1 collective-permute-start.2
  33.0 0.7 shard_map.130.refs_0_
  33.7 1.2 %collective-permute-done.2.refs_1_ = bf16[144,2048]{1,0:T(8,128)(2,1)S(1)} collective-permute-done((bf16[144,2048]{1,0:T(8,128)(2,1)S(1)}, bf16[144,2048]{1,0:T(8,128)(2,1)S(1)}, u32[]{:S(2)}, u32[]{:S(2)}) %collective-permute-start.2) | collective-permute-done | bytes 589856 | tf_op jit(solution)/shard_map/ppermute | solution.py:41
  35.0 0.0 copy-done
  35.0 0.7 shard_map.131
  35.6 31.7 %all_to_all.10.refs_0_ = bf16[16,112,256]{2,1,0:T(8,128)(2,1)S(1)} all-to-all(bf16[16,112,256]{2,1,0:T(8,128)(2,1)S(1)} %get-tuple-element.29), channel_id=1, replica_groups=mesh['seq'=16,'exp'=2] {'seq'}, dimensions={0} | all-to-all | bytes 1835008 | tf_op jit(solution)/shard_map/all_to_all | solution.py:726
  67.3 0.0 collective-permute-start.3
  67.3 0.0 copy-done.3
  67.3 4.8 %shard_map.132 = (f32[2,112,1408]{2,1,0:T(8,128)S(1)}, f32[2,112,1408]{2,1,0:T(8,128)S(1)}, f32[2,112,128]{2,1,0:T(8,128)S(1)}) custom-call(bf16[16,112,256]{2,1,0:T(8,128)(2,1)S(1)} %all_to_all.10.refs_0_, bf16[7,448,256]{2,1,0:T(8,128)(2,1)S(1)} %get-tuple-element.30.refs_1_.refs_2_, f32[1,2048]{1,0:T(1,128)S(1)} %bitcast.7, bf16[2,4096]{1,0:T(2,128)(2,1)S(1)} %bitcast.8, ...), custom_call_target="tpu_custom_call" | custom-call | flops 2583691264 | bytes 23068672 | tf_op jit(solution)/shard_map/pallas_call | solution.py:51
  72.1 0.0 collective-permute-done.3.refs_0_
  72.1 14.5 %shard_map.133 = (bf16[2,112,1408]{2,1,0:T(8,128)(2,1)S(1)}, bf16[16,112,256]{2,1,0:T(8,128)(2,1)S(1)}) custom-call(bf16[16,112,256]{2,1,0:T(8,128)(2,1)S(1)} %collective-permute-done.3.refs_0_, bf16[144,2048]{1,0:T(8,128)(2,1)S(1)} %collective-permute-done.2.refs_1_, bf16[7,448,256]{2,1,0:T(8,128)(2,1)S(1)} %get-tuple-element.30.refs_1_.refs_2_, ...), custom_call_target="tpu_custom_call" | custom-call | flops 3875536896 | bytes 34603008 | tf_op jit(solution)/shard_map/pallas_call | solution.py:51
  86.6 0.6 collective-permute-start.4
  87.2 6.0 %shard_map.134.refs_0_ = bf16[16,112,256]{2,1,0:T(8,128)(2,1)S(1)} custom-call(bf16[2,112,1408]{2,1,0:T(8,128)(2,1)S(1)} %get-tuple-element.39.hidden_ref, bf16[7,256,448]{2,1,0:T(8,128)(2,1)S(1)} %get-tuple-element.31.refs_3_.spread_ref, bf16[2,1408,4096]{2,1,0:T(8,128)(2,1)} %down_ref.1), custom_call_target="tpu_custom_call" | custom-call | flops 1291845632 | bytes 11534336 | tf_op jit(solution)/shard_map/pallas_call | solution.py:51
  93.1 0.0 collective-permute-done.4.refs_1_
  93.1 0.2 shard_map.135
  93.4 27.4 %all_to_all.11.returned_ref = bf16[16,112,256]{2,1,0:T(8,128)(2,1)S(1)} all-to-all(bf16[16,112,256]{2,1,0:T(8,128)(2,1)S(1)} %shard_map.135), channel_id=1, replica_groups=mesh['seq'=16,'exp'=2] {'seq'}, dimensions={0} | all-to-all | bytes 1835008 | tf_op jit(solution)/shard_map/all_to_all | solution.py:726
  120.8 1.3 %shard_map.136 = bf16[128,2048]{1,0:T(8,128)(2,1)} custom-call(f32[128,2048]{1,0:T(8,128)S(1)} %get-tuple-element.28.residual_ref, bf16[16,112,256]{2,1,0:T(8,128)(2,1)S(1)} %all_to_all.11.returned_ref, bf16[8,256,128]{2,1,0:T(8,128)(2,1)S(1)} %get-tuple-element.27.refs_4_.places_ref), custom_call_target="tpu_custom_call" | custom-call | tf_op jit(solution)/shard_map/pallas_call | solution.py:51
  (2 shorter events, 0.0 us)
Async XLA Ops:
  1.1 28.7 %collective-permute-start.1 = (bf16[272,1024]{1,0:T(8,128)(2,1)S(1)}, bf16[272,1024]{1,0:T(8,128)(2,1)S(1)}, u32[]{:S(2)}, u32[]{:S(2)}) collective-permute-start(bf16[272,1024]{1,0:T(8,128)(2,1)S(1)} %shard_map.127.refs_1_), channel_id=1, source_target_pairs={{0,4},{2,6},{4,8},{6,10},{8,12},{10,14},{12,16},{14,18},{16,20},{1... | collective-permute-start | bytes 1671176 | tf_op jit(solution)/shard_map/ppermute | solution.py:36
  6.0 23.8 %collective-permute-start = (bf16[272,1024]{1,0:T(8,128)(2,1)S(1)}, bf16[272,1024]{1,0:T(8,128)(2,1)S(1)}, u32[]{:S(2)}, u32[]{:S(2)}) collective-permute-start(bf16[272,1024]{1,0:T(8,128)(2,1)S(1)} %shard_map.127.refs_1_), channel_id=1, source_target_pairs={{0,2},{2,4},{4,6},{6,8},{8,10},{10,12},{12,14},{14,16},{16,18},{18... | collective-permute-start | bytes 1671176 | tf_op jit(solution)/shard_map/ppermute | solution.py:36
  9.4 0.7 copy-start.4
  10.1 0.7 copy-start.5
  10.7 19.0 %copy-start.1 = (bf16[128,1024]{1,0:T(8,128)(2,1)S(1)}, bf16[128,1024]{1,0:T(8,128)(2,1)}, u32[]{:S(2)}) copy-start(bf16[128,1024]{1,0:T(8,128)(2,1)} %refs_0_.3) | copy-start | bytes 786436
  10.7 19.0 %copy-start.2 = (f32[2048]{0:T(1024)S(1)}, f32[2048]{0:T(1024)}, u32[]{:S(2)}) copy-start(f32[2048]{0:T(1024)} %param.19) | copy-start | bytes 24580
  21.8 13.1 %copy-start = (bf16[128,2048]{1,0:T(8,128)(2,1)S(1)}, bf16[128,2048]{1,0:T(8,128)(2,1)}, u32[]{:S(2)}) copy-start(bf16[128,2048]{1,0:T(8,128)(2,1)} %refs_2_.3) | copy-start | bytes 1572868
  32.9 34.5 %copy-start.3 = (bf16[4096,2]{0,1:T(2,128)(2,1)S(1)}, bf16[4096,2]{0,1:T(2,128)(2,1)}, u32[]{:S(2)}) copy-start(bf16[4096,2]{0,1:T(2,128)(2,1)} %param.20) | copy-start | bytes 49156
  32.9 2.1 %collective-permute-start.2 = (bf16[144,2048]{1,0:T(8,128)(2,1)S(1)}, bf16[144,2048]{1,0:T(8,128)(2,1)S(1)}, u32[]{:S(2)}, u32[]{:S(2)}) collective-permute-start(bf16[144,2048]{1,0:T(8,128)(2,1)S(1)} %get-tuple-element.26), channel_id=1, source_target_pairs={{0,1},{1,0},{2,3},{3,2},{4,5},{5,4},{6,7},{7,6},{8,9},{9,8},{10,11... | collective-permute-start | bytes 1769480 | tf_op jit(solution)/shard_map/ppermute | solution.py:41
  67.3 4.8 %collective-permute-start.3 = (bf16[16,112,256]{2,1,0:T(8,128)(2,1)S(1)}, bf16[16,112,256]{2,1,0:T(8,128)(2,1)S(1)}, u32[]{:S(2)}, u32[]{:S(2)}) collective-permute-start(bf16[16,112,256]{2,1,0:T(8,128)(2,1)S(1)} %all_to_all.10.refs_0_), channel_id=1, source_target_pairs={{0,1},{1,0},{2,3},{3,2},{4,5},{5,4},{6,7},{7,6},{8,9},{9,8},{10,11... | collective-permute-start | bytes 2752520 | tf_op jit(solution)/shard_map/ppermute | solution.py:41
  86.6 6.5 %collective-permute-start.4 = (bf16[16,112,256]{2,1,0:T(8,128)(2,1)S(1)}, bf16[16,112,256]{2,1,0:T(8,128)(2,1)S(1)}, u32[]{:S(2)}, u32[]{:S(2)}) collective-permute-start(bf16[16,112,256]{2,1,0:T(8,128)(2,1)S(1)} %get-tuple-element.40), channel_id=1, source_target_pairs={{0,1},{1,0},{2,3},{3,2},{4,5},{5,4},{6,7},{7,6},{8,9},{9,8},{10,11... | collective-permute-start | bytes 2752520 | tf_op jit(solution)/shard_map/ppermute | solution.py:41
